TPU v7x, 128 devices: a whole 4x4x4 slice. The times are simulated.
128 devices in a mesh: dp: 8 (over x, core), mp: 16 (over z, y).
Axes of the slice: x: 4, y: 4, z: 4, core: 2. Of those that a mesh axis runs over, the one named last changes fastest.
Arguments:
- queries: bfloat16 [1024, 4096], P('dp', 'mp'), may hold values from -48 to 48
- passages: bfloat16 [1024, 4096], P('dp', 'mp'), may hold values from -12 to 12
- pool_rows: bfloat16 [65536, 4096], P(('dp', 'mp')), may hold values from -6 to 6
- negatives: int32 [1024, 31], P(('dp', 'mp')), may hold values from 0 to 65535, as said below
Outputs:
- mean_loss: float32 [], replicated
- grad_queries: bfloat16 [1024, 4096], P('dp', 'mp')
- grad_passages: bfloat16 [1024, 4096], P('dp', 'mp')
- grad_pool: bfloat16 [65536, 4096], P(('dp', 'mp'))
Inputs may be any that keep to these rules, and one draw needn't show every extreme that they name: `negatives`: row r of the pool lies on device r // 512 in dp+mp order. Among the 248 pairs of one device's queries, at most 4 name rows of one device; in every draw some device is named by exactly 4 pairs of every device's queries. A query may name one row more than once.
All inputs are finite; a program needn't handle non-finite values.
Results may differ from a plain program's by a relative error of at most 0.017.
Values may be sent and summed in bfloat16 or wider, within the bound.
A program may use at most 128 MiB of HBM per device.

v0:
```python
import math

import jax
import jax.numpy as jnp
from jax import lax
from jax.sharding import PartitionSpec as P

D = 4096


def body(queries, passages, pool_rows, negatives):
    inverse_square_root = 1.0 / math.sqrt(D)
    n_dp = lax.axis_size("dp")
    n_mp = lax.axis_size("mp")
    n_all = n_dp * n_mp
    q_dev = queries.shape[0]
    qrows = q_dev // n_mp
    neg_count = negatives.shape[1]
    pool_dev = pool_rows.shape[0]
    width_full = pool_rows.shape[1]
    slots = max(2, 12 * qrows * neg_count // (5 * n_all))
    gathered = lax.all_gather(passages, "dp", axis=0, tiled=True)
    batch_total = gathered.shape[0]
    inbatch = (
        lax.psum_scatter(
            lax.dot_general(
                queries, gathered, (((1,), (1,)), ((), ())), preferred_element_type=jnp.float32
            ),
            "mp",
            scatter_dimension=0,
            tiled=True,
        )
        * inverse_square_root
    )
    complete_query = lax.all_to_all(queries, "mp", split_axis=0, concat_axis=1, tiled=True)
    flat_ids = negatives.reshape(-1)
    owners = flat_ids // pool_dev
    local_ids = flat_ids - owners * pool_dev
    owner_hits = (owners[:, None] == jnp.arange(n_all)[None, :]).astype(jnp.int32)
    earlier_hits = jnp.cumsum(owner_hits, axis=0) - owner_hits
    slot_of = jnp.sum(earlier_hits * owner_hits, axis=1)
    requests = jnp.zeros((n_all, slots), jnp.int32).at[owners, slot_of].set(local_ids)
    incoming = lax.all_to_all(requests, ("dp", "mp"), split_axis=0, concat_axis=0, tiled=True)
    received_rows = lax.all_to_all(
        jnp.take(pool_rows, incoming, axis=0), ("dp", "mp"), split_axis=0, concat_axis=0, tiled=True
    )
    paired_row_scores = received_rows[owners, slot_of].reshape(qrows, neg_count, width_full)
    hard = (
        jnp.einsum(
            "oa,ofa->of", complete_query, paired_row_scores, preferred_element_type=jnp.float32
        )
        * inverse_square_root
    )
    logits = jnp.concatenate([inbatch, hard], axis=1)
    highest = jnp.max(logits, axis=1, keepdims=True)
    log_total = highest + jnp.log(jnp.sum(jnp.exp(logits - highest), axis=1, keepdims=True))
    first_query = lax.axis_index("dp") * q_dev + lax.axis_index("mp") * qrows
    query_ids = first_query + jnp.arange(qrows)
    positive_mask = (jnp.arange(batch_total)[None, :] == query_ids[:, None]).astype(jnp.float32)
    positive = jnp.sum(inbatch * positive_mask, axis=1)
    loss_sum = lax.psum(jnp.sum(log_total[:, 0] - positive), ("dp", "mp"))
    mean_loss = loss_sum / batch_total
    probs = jnp.exp(logits - log_total)
    grad_inbatch = ((probs[:, :batch_total] - positive_mask) / batch_total).astype(jnp.bfloat16)
    gradient_hard_negatives = (probs[:, batch_total:] / batch_total).astype(jnp.bfloat16)
    grad_group = lax.all_gather(grad_inbatch, "mp", axis=0, tiled=True)
    inbatch_part = jnp.dot(grad_group, gathered, preferred_element_type=jnp.float32)
    grad_passages = (
        lax.psum_scatter(
            lax.dot_general(
                grad_group, queries, (((0,), (0,)), ((), ())), preferred_element_type=jnp.float32
            ),
            "dp",
            scatter_dimension=0,
            tiled=True,
        )
        * inverse_square_root
    ).astype(jnp.bfloat16)
    query_hard_scores = jnp.einsum(
        "ei,eic->ec", gradient_hard_negatives, paired_row_scores, preferred_element_type=jnp.float32
    )
    hard_slices = lax.all_to_all(
        query_hard_scores.astype(jnp.bfloat16), "mp", split_axis=1, concat_axis=0, tiled=True
    ).astype(query_hard_scores.dtype)
    grad_queries = ((inbatch_part + hard_slices) * inverse_square_root).astype(jnp.bfloat16)
    repeated = jnp.repeat(complete_query, neg_count, axis=0)
    pair_terms = (
        gradient_hard_negatives.reshape(-1).astype(jnp.float32)[:, None]
        * repeated.astype(jnp.float32)
        * inverse_square_root
    ).astype(jnp.bfloat16)
    outbound = (
        jnp.zeros((n_all, slots, width_full), jnp.bfloat16).at[owners, slot_of].set(pair_terms)
    )
    arrived = lax.all_to_all(outbound, ("dp", "mp"), split_axis=0, concat_axis=0, tiled=True)
    accum = jnp.zeros((pool_dev, width_full), jnp.float32)
    accum = accum.at[incoming.reshape(-1)].add(arrived.reshape(-1, width_full).astype(jnp.float32))
    grad_pool = accum.astype(jnp.bfloat16)
    return (mean_loss, grad_queries, grad_passages, grad_pool)


def solution(mesh):
    placed = (P("dp", "mp"), P("dp", "mp"), P(("dp", "mp"), None), P(("dp", "mp"), None))
    return jax.shard_map(
        body,
        mesh=mesh,
        in_specs=placed,
        out_specs=(P(), P("dp", "mp"), P("dp", "mp"), P(("dp", "mp"), None)),
        check_vma=False,
    )
```

profile of v0, /device:TPU:1, one launch (start us, length us, event | category | flops | bytes accessed | tf_op | source)
XLA Modules:
  0.0 493.3 jit_solution(3916240725024034839)
XLA Ops:
  7.2 0.8 reshape.237
  7.9 0.8 reshape.236
  8.7 0.1 iota_compare_fusion
  8.8 0.1 fusion.6
  9.1 0.2 fusion.9
  9.3 12.2 %scatter_fusion = s32[128,4]{0,1:T(4,128)S(1)} fusion(s32[128,4]{0,1:T(4,128)S(1)} %broadcast_in_dim.20, s32[248]{0:T(256)S(1)} %bitcast.51, s32[248]{0:T(256)S(1)} %get-tuple-element.8), kind=kCustom, calls=%fused_computation.2 | custom fusion | bytes 4960 | tf_op jit(solution)/shard_map/scatter | solution.py:42
  21.5 0.1 copy.16
  21.6 21.1 %all_to_all.57 = s32[128,1,4]{2,1,0:T(1,128)S(1)} all-to-all(s32[128,1,4]{2,1,0:T(1,128)S(1)} %copy.16), channel_id=1, replica_groups=mesh['dp'=8,'mp'=16] {'dp','mp'}, dimensions={0} | all-to-all | bytes 4096 | tf_op jit(solution)/shard_map/all_to_all | solution.py:43
  42.7 3.5 all-to-all-start.2
  46.3 0.1 copy.18
  46.5 0.1 reshape.248
  46.6 11.3 %gather_fusion = bf16[512,4096]{1,0:T(8,128)(2,1)} fusion(bf16[512,4096]{1,0:T(8,128)(2,1)} %param.6, s32[1024]{0:T(1024)S(1)} %pad_clamp_fusion), kind=kCustom, calls=%fused_computation | custom fusion | bytes 8390656 | tf_op jit(solution)/shard_map/jit(_take)/gather | solution.py:45
  57.9 7.2 %reshape.247 = bf16[128,4,4096]{2,1,0:T(4,128)(2,1)} reshape(bf16[512,4096]{1,0:T(8,128)(2,1)} %gather_fusion) | data formatting | bytes 8388608 | tf_op jit(solution)/shard_map/jit(_take)/gather | solution.py:45
  65.1 6.3 %broadcast_select_fusion = bf16[128,4,4096]{2,1,0:T(4,128)(2,1)} fusion(bf16[128,4,4096]{2,1,0:T(4,128)(2,1)} %reshape.247, pred[128,4]{1,0:T(8,128)(4,1)S(1)} %copy.18), kind=kLoop, calls=%fused_computation.7 | loop fusion | flops 2097152 | bytes 8389120 | tf_op jit(solution)/shard_map/jit(_take)/select_n | solution.py:45
  71.4 8.5 %all-to-all-start.1 = ((bf16[128,4,4096]{2,1,0:T(4,128)(2,1)}), bf16[128,4,4096]{2,1,0:T(4,128)(2,1)}, u32[]{:S(2)}, u32[]{:S(2)}) async-start(bf16[128,4,4096]{2,1,0:T(4,128)(2,1)} %broadcast_select_fusion), calls=%async_computation.1 | async-start | bytes 8388608 | tf_op jit(solution)/shard_map/all_to_all | solution.py:44
  79.9 55.9 %all_gather.6 = bf16[1024,256]{1,0:T(8,128)(2,1)S(1)} all-gather(bf16[128,256]{1,0:T(8,128)(2,1)S(1)} %copy-done.1), channel_id=1, replica_groups=mesh['dp'=8,'mp'=16] {'dp'}, dimensions={0}, use_global_device_ids=true | all-gather | bytes 589824 | tf_op jit(solution)/shard_map/all_gather | solution.py:22
  135.8 1.2 fusion.20
  137.0 0.6 dynamic-slice
  138.3 2.4 broadcast_in_dim.44
  140.7 4.6 convert_element_type.73
  145.3 75.4 %all-reduce.4.cloned.1.call-done = f32[128,1024]{1,0:T(8,128)} async-done(((f32[128,1024]{1,0:T(8,128)}), f32[128,1024]{1,0:T(8,128)}) %all-reduce.4.cloned.1.call-update) | async-done | bytes 524304
  220.7 1.0 select_reduce_fusion
  221.7 7.9 %gather_fusion.1 = bf16[248,4096]{1,0:T(8,128)(2,1)} fusion(bf16[128,4,4096]{2,1,0:T(4,128)(2,1)} %all-to-all-done.1, s32[248]{0:T(256)S(1)} %bitcast.53), kind=kCustom, calls=%fused_computation.1 | custom fusion | bytes 4065216 | tf_op jit(solution)/shard_map/gather | solution.py:47
  229.6 2.2 reshape.240
  231.8 0.6 fusion.4
  232.5 0.1 broadcast_multiply_fusion
  232.6 0.2 exponential_reduce_fusion
  232.8 0.6 subtract_reduce_fusion
  233.4 0.1 subtract_exponential_fusion
  233.5 0.4 fusion.13
  233.9 0.7 copy.30
  234.6 0.1 reshape.244
  234.7 4.3 all-to-all-start.3
  239.0 2.7 multiply_convert_fusion
  241.7 4.1 broadcast_in_dim.43
  245.8 61.1 %scatter_fusion.1 = bf16[128,4,4096]{2,1,0:T(4,128)(2,1)} fusion(bf16[128,4,4096]{2,1,0:T(4,128)(2,1)} %broadcast_in_dim.43, s32[248]{0:T(256)S(1)} %bitcast.52, bf16[248,4096]{1,0:T(8,128)(2,1)S(1)} %multiply_convert_fusion), kind=kCustom, calls=%fused_computation.3 | custom fusion | bytes 6096832 | tf_op jit(solution)/shard_map/scatter | solution.py:93
  306.8 12.6 %all-to-all-start.4 = ((bf16[128,4,4096]{2,1,0:T(4,128)(2,1)}), bf16[128,4,4096]{2,1,0:T(4,128)(2,1)}, u32[]{:S(2)}, u32[]{:S(2)}) async-start(bf16[128,4,4096]{2,1,0:T(4,128)(2,1)} %scatter_fusion.1), calls=%async_computation.5 | async-start | bytes 8388608 | tf_op jit(solution)/shard_map/all_to_all | solution.py:95
  319.6 59.8 %all_gather.7 = bf16[128,1024]{1,0:T(8,128)(2,1)S(1)} all-gather(bf16[8,1024]{1,0:T(8,128)(2,1)S(1)} %fusion.11), channel_id=1, replica_groups=mesh['dp'=8,'mp'=16] {'mp'}, dimensions={0}, use_global_device_ids=true | all-gather | bytes 278528 | tf_op jit(solution)/shard_map/all_gather | solution.py:66
  379.4 1.3 fusion.21
  380.7 0.5 broadcast.254
  381.2 0.8 reduce.5
  382.0 0.1 reshape.241
  382.1 68.5 %psum.7 = f32[]{:T(128)} all-reduce(f32[]{:T(128)} %get-tuple-element.6), channel_id=1, replica_groups=mesh['dp'=8,'mp'=16] {'dp','mp'}, use_global_device_ids=true, to_apply=%region_10.11 | all-reduce | flops 1 | bytes 8 | tf_op jit(solution)/shard_map/psum | solution.py:61
  451.3 0.9 fusion.3
  452.1 1.5 multiply_convert_fusion.1
  453.7 7.3 %reshape.276 = f32[512,4096]{1,0:T(8,128)} reshape(bf16[128,4,4096]{2,1,0:T(4,128)(2,1)} %all-to-all-done.4) | data formatting | bytes 12582912 | tf_op jit(solution)/shard_map/convert_element_type | solution.py:97
  460.9 17.9 %scatter_custom_fusion.2 = f32[512,4096]{1,0:T(8,128)} fusion(s32[512]{0:T(512)S(1)} %bitcast.65, f32[512,4096]{1,0:T(8,128)} %reshape.276, f32[]{:T(128)} %constant.71.clone.1), kind=kCustom, calls=%fused_computation.5 | custom fusion | flops 2097152 | bytes 8389120 | tf_op jit(solution)/shard_map/scatter-add | solution.py:97
  478.8 6.0 %convert_element_type.77 = bf16[512,4096]{1,0:T(8,128)(2,1)} convert(f32[512,4096]{1,0:T(8,128)} %scatter_custom_fusion.2) | non-fusion elementwise | flops 2097152 | bytes 12582912 | tf_op jit(solution)/shard_map/convert_element_type | solution.py:98
  (34 shorter events, 0.5 us)
Async XLA Ops:
  42.7 28.7 %all-to-all-start.2 = ((bf16[16,8,256]{2,1,0:T(8,128)(2,1)}), bf16[16,8,256]{2,1,0:T(8,128)(2,1)S(1)}, u32[]{:S(2)}, u32[]{:S(2)}) async-start(bf16[16,8,256]{2,1,0:T(8,128)(2,1)} %bitcast.55), calls=%async_computation.2 | async-start | bytes 131072 | tf_op jit(solution)/shard_map/all_to_all | solution.py:35
  71.4 8.5 %copy-start.1 = (bf16[128,256]{1,0:T(8,128)(2,1)S(1)}, bf16[128,256]{1,0:T(8,128)(2,1)}, u32[]{:S(2)}) copy-start(bf16[128,256]{1,0:T(8,128)(2,1)} %param.5) | copy-start | bytes 196612
  71.4 64.4 %copy-start = (bf16[128,256]{1,0:T(8,128)(2,1)S(1)}, bf16[128,256]{1,0:T(8,128)(2,1)}, u32[]{:S(2)}) copy-start(bf16[128,256]{1,0:T(8,128)(2,1)} %param.4) | copy-start | bytes 196612
  71.4 65.6 %copy-start.2 = (u32[128]{0:T(128)S(1)}, u32[128]{0:T(128)}, u32[]{:S(2)}) copy-start(u32[128]{0:T(128)} %constant.128) | copy-start | bytes 1540
  71.4 150.3 %all-to-all-start.1 = ((bf16[128,4,4096]{2,1,0:T(4,128)(2,1)}), bf16[128,4,4096]{2,1,0:T(4,128)(2,1)}, u32[]{:S(2)}, u32[]{:S(2)}) async-start(bf16[128,4,4096]{2,1,0:T(4,128)(2,1)} %broadcast_select_fusion), calls=%async_computation.1 | async-start | bytes 8388608 | tf_op jit(solution)/shard_map/all_to_all | solution.py:44
  79.9 140.9 %all-reduce.4.cloned.1.call-start = ((), (), s32[]{:S(2)}) async-start(), calls=%async_computation.7 | async-start | bytes 1048576
  234.7 72.2 %all-to-all-start.3 = ((bf16[8,16,256]{2,0,1:T(8,128)(2,1)}), bf16[8,16,256]{2,0,1:T(8,128)(2,1)S(1)}, u32[]{:S(2)}, u32[]{:S(2)}) async-start(bf16[8,16,256]{2,0,1:T(8,128)(2,1)} %bitcast.18), calls=%async_computation.3 | async-start | bytes 131072 | tf_op jit(solution)/shard_map/all_to_all | solution.py:82
  306.8 146.8 %all-to-all-start.4 = ((bf16[128,4,4096]{2,1,0:T(4,128)(2,1)}), bf16[128,4,4096]{2,1,0:T(4,128)(2,1)}, u32[]{:S(2)}, u32[]{:S(2)}) async-start(bf16[128,4,4096]{2,1,0:T(4,128)(2,1)} %scatter_fusion.1), calls=%async_computation.5 | async-start | bytes 8388608 | tf_op jit(solution)/shard_map/all_to_all | solution.py:95
  319.4 132.7 %reduce-scatter.2.cloned.1.call-start = ((), (), s32[]{:S(2)}) async-start(), calls=%async_computation.6 | async-start | bytes 1179648 | tf_op jit(solution)/shard_map/reduce_scatter | solution.py:69
Sparse Core Ops, SparseCore 0:
  137.1 83.5 all-reduce.3
  380.8 33.9 reduce-scatter.1
where the time goes:
time: 503 us; the launch traced here: 493 us
  blocking collectives  205 us (41%)
  local copies, waits for them, and re-layouts  124 us (25%)
  waiting for transfers between devices  75.5 us (15%)
  other arithmetic  37.9 us (8%)
  starting transfers between devices  28.9 us (6%)
  between operations  17.1 us (3%)
    unnamed x3, waiting for transfers between devices  75.5 us
    psum x1, blocking collectives, body(): loss_sum = lax.psum(jnp.sum(log_total[:, 0] - positive), ('dp', 'mp'))  68.5 us
    scatter x1, local copies, waits for them, and re-layouts, body(): jnp.zeros((n_all, slots, width_full), jnp.bfloat16).at[owners, slot_of]  61.1 us
    all_gather x1, blocking collectives, body(): grad_group = lax.all_gather(grad_inbatch, 'mp', axis=0, tiled=True)  59.8 us
    all_gather x1, blocking collectives, body(): gathered = lax.all_gather(passages, 'dp', axis=0, tiled=True)  55.9 us
    all_to_all x1, blocking collectives, body(): lax.all_to_all(requests, ('dp', 'mp'), split_axis=0, concat_axis=0, tiled...  21.1 us
    gather x2, local copies, waits for them, and re-layouts, body(): jnp.take(pool_rows, incoming, axis=0)  18.5 us
    scatter-add x1, other arithmetic, body(): accum.at[incoming.reshape(-1)]  17.9 us
  transfers between devices with their start and end apart: 6, of which 1 were waited for; matrix products, arithmetic and copies ran while one was open for 22% of the time, Pallas kernels for 0%

commit v1 on v0

v1 whole, which is shorter than its diff:
```python
import jax
import jax.numpy as jnp
from jax import lax
from jax.experimental import pallas as pl
from jax.experimental.pallas import tpu as pltpu
from jax.sharding import PartitionSpec as P

MESH = pl.DeviceIdType.MESH
F32 = jnp.float32
BF16 = jnp.bfloat16

D = 4096
NEGS = 31
BATCH = 1024
ROWS = 512
PLANE = 512
SCALE = 1.0 / 64.0
ORDERS = ("xyz", "yzx", "zxy")
PART_OFF = (0, 48, 96)
AG_ROWS = 48
RS_ROWS = (48, 48, 32)
LOW = -1e30


def kernel(
    q_ref, p_ref, pool_ref, neg_ref,
    loss_ref, gq_ref, gp_ref, gpool_ref,
    ag0, ag1, ag2, pool, queries, pas_rx, pas, scores, pscores, names, et, pet, wd, wx, fcol,
    stats, loss_own, loss_sib, gp_tx, gp_rx, out,
    d0, d1, d2,
    h0a, h0b, h0c, h0d, f0a, f0b, f0c, f0d, i0a, i0b, g0a, g0b,
    h1a, h1b, h1c, h1d, f1a, f1b, f1c, f1d, i1a, i1b, g1a, g1b,
    h2a, h2b, h2c, h2d, f2a, f2b, f2c, f2d, i2a, i2b, g2a, g2b,
    local_sem, pool_send, pool_recv, ag_send, ag_recv, pas_send, pas_recv, q_send, q_recv,
    st_send, st_recv, w_send, w_recv, rs_send, rs_recv, gp_send, gp_recv, loss_send, loss_recv, out_sem,
):
    dp = lax.axis_index("dp")
    mp = lax.axis_index("mp")
    core = lax.rem(dp, 2)
    at = {"x": dp // 2, "y": lax.rem(mp, 4), "z": mp // 4}
    zy = mp
    sib = (at["x"] * 2 + 1 - core, mp)

    def peer(axis, delta):
        there = dict(at)
        there[axis] = lax.rem(at[axis] + delta, 4)
        return (there["x"] * 2 + core, there["z"] * 4 + there["y"])

    def send(src, dst, send_sem, recv_sem, device):
        copy = pltpu.make_async_remote_copy(
            src_ref=src, dst_ref=dst, send_sem=send_sem, recv_sem=recv_sem,
            device_id=device, device_id_type=MESH,
        )
        copy.start()
        return copy

    def arrived(ref, sem):
        pltpu.make_async_copy(ref, ref, sem).wait()

    barrier = pltpu.get_barrier_semaphore()
    for axis in "xyz":
        for delta in (1, 3):
            pl.semaphore_signal(barrier, inc=1, device_id=peer(axis, delta), device_id_type=MESH)
    pl.semaphore_signal(barrier, inc=1, device_id=sib, device_id_type=MESH)
    pl.semaphore_wait(barrier, 7)

    pending = []

    ags = (ag0, ag1, ag2)

    def slot(part):
        a, b, c = ORDERS[part]
        return at[c], at[b], at[a]

    c, b, a = slot(0)
    ag0[c, b, a] = q_ref[0:48, :]
    c, b, a = slot(1)
    ag1[c, b, a] = q_ref[48:96, :]
    c, b, a = slot(2)
    ag2[c, b, a, 0:32] = q_ref[96:128, :]
    ids = neg_ref[...]
    high = (ids >> 8).astype(F32)
    low = (ids & 255).astype(F32)
    ag2[c, b, a, 32:48] = jnp.concatenate([high, low], axis=0).astype(BF16)

    def ag_blocks(part, phase):
        buf = ags[part]
        c, b, a = slot(part)
        if phase == 0:
            return lambda g: buf.at[c, b, g], lambda g, h: buf.at[c, b, g, :, 128 * h : 128 * h + 128]
        if phase == 1:
            return lambda g: buf.at[c, g], lambda g, h: buf.at[c, g, 2 * h : 2 * h + 2]
        return lambda g: buf.at[g], lambda g, h: buf.at[g, 2 * h : 2 * h + 2]

    def ag_phase(phase):
        views = []
        for part in range(3):
            axis = ORDERS[part][phase]
            block, half = ag_blocks(part, phase)
            g = at[axis]
            k = (part * 3 + phase) * 4
            right, left = peer(axis, 1), peer(axis, 3)
            pending.append(send(block(g), block(g), ag_send.at[k], ag_recv.at[k], right))
            pending.append(send(block(g), block(g), ag_send.at[k + 1], ag_recv.at[k + 1], left))
            views.append((block, half, g, k, right, left))
        for block, half, g, k, right, left in views:
            before, after = lax.rem(g + 3, 4), lax.rem(g + 1, 4)
            arrived(block(before), ag_recv.at[k])
            pending.append(send(half(before, 0), half(before, 0), ag_send.at[k + 2], ag_recv.at[k + 2], right))
            arrived(block(after), ag_recv.at[k + 1])
            pending.append(send(half(after, 1), half(after, 1), ag_send.at[k + 3], ag_recv.at[k + 3], left))
        for block, half, g, k, right, left in views:
            far = lax.rem(g + 2, 4)
            arrived(half(far, 0), ag_recv.at[k + 2])
            arrived(half(far, 1), ag_recv.at[k + 3])

    ag_phase(0)
    own_pool = pltpu.make_async_copy(pool_ref, pool.at[0:ROWS], local_sem)
    own_pool.start()
    pool_copy = send(pool_ref, pool.at[ROWS : 2 * ROWS], pool_send, pool_recv, sib)
    ag_phase(1)

    for t in range(8):
        for other in range(2):
            chip = core * 8 + t
            target = (at["x"] * 2 + other, chip)
            me = jnp.logical_and(chip == zy, core == other)
            src = p_ref.at[16 * t : 16 * t + 16]
            dst = pas_rx.at[zy]
            k = t * 2 + other

            @pl.when(me)
            def _():
                pltpu.make_async_copy(src, dst, pas_recv.at[zy]).start()

            @pl.when(jnp.logical_not(me))
            def _():
                send(src, dst, pas_send.at[k], pas_recv.at[zy], target)

    ag_phase(2)

    def assemble(i, _):
        z, y = i // 4, lax.rem(i, 4)
        cols = pl.ds(pl.multiple_of(i * 256, 256), 256)
        for x in range(4):
            where = {"x": x, "y": y, "z": z}
            for part in range(3):
                aa, bb, cc = ORDERS[part]
                rows = RS_ROWS[part]
                start = x * 128 + PART_OFF[part]
                queries[start : start + rows, cols] = ags[part][where[cc], where[bb], where[aa], 0:rows]
        return 0

    lax.fori_loop(0, 16, assemble, 0)
    q_copy = send(queries.at[0:PLANE], queries.at[PLANE : 2 * PLANE], q_send, q_recv, sib)

    for i in range(16):
        arrived(pas_rx.at[i], pas_recv.at[i])
        pas[:, 256 * i : 256 * i + 256] = pas_rx[i]

    mine = dp * 16 + mp
    theirs = (at["x"] * 2 + 1 - core) * 16 + mp
    sub = lax.broadcasted_iota(jnp.int32, (128, 128), 0)
    for x in range(4):
        pieces = []
        for i in range(16):
            where = {"x": x, "y": i % 4, "z": i // 4}
            aa, bb, cc = ORDERS[2]
            tile = ag2[where[cc], where[bb], where[aa], 32:48, 0:128].astype(F32)
            pieces.append(tile[0:8] * 256.0 + tile[8:16])
        named = jnp.concatenate(pieces, axis=0).T[0:32].astype(jnp.int32)
        owner = named >> 9
        field = ((named >> 7) & 3) * 4
        bit = jnp.where(
            owner == mine, jnp.left_shift(1, field),
            jnp.where(owner == theirs, jnp.left_shift(1, field + 16), 0),
        )
        hi = named & 127
        packed = jnp.zeros((128, 128), jnp.int32)
        for k in range(NEGS):
            packed = packed + jnp.where(sub == hi[k : k + 1], bit[k : k + 1], 0)
        names[:, 128 * x : 128 * x + 128] = packed

    own_pool.wait()
    pool_copy.wait_recv()
    contract = (((1,), (1,)), ((), ()))
    scores[...] = jnp.zeros_like(scores)

    def score(i, _):
        cols = pl.ds(pl.multiple_of(i * 1024, 1024), 1024)
        scores[...] += lax.dot_general(pool[:, cols], queries[0:PLANE, cols], contract, preferred_element_type=F32)
        return 0

    lax.fori_loop(0, 4, score, 0)
    ps = lax.dot_general(pas[...], queries[0:PLANE, :], contract, preferred_element_type=F32) * SCALE

    lane = lax.broadcasted_iota(jnp.int32, (16, PLANE), 1)
    psub = lax.broadcasted_iota(jnp.int32, (16, PLANE), 0)
    in_plane = core == zy // 8
    first = jnp.where(in_plane, at["x"] * 128 + lax.rem(zy, 8) * 16, -1024)
    same = lane == first + psub
    pos = jnp.sum(jnp.where(same, ps, 0.0), axis=0, keepdims=True)

    def count_of(f):
        return (names[...] >> (4 * f)) & 15

    top = jnp.max(ps, axis=0, keepdims=True)
    for f in range(8):
        s = jnp.where(count_of(f) > 0, scores[128 * f : 128 * f + 128] * SCALE, LOW)
        scores[128 * f : 128 * f + 128] = s
        top = jnp.maximum(top, jnp.max(s, axis=0, keepdims=True))
    pe = jnp.exp(ps - top)
    pscores[...] = pe
    total = jnp.sum(pe, axis=0, keepdims=True)
    for f in range(8):
        e = jnp.exp(scores[128 * f : 128 * f + 128] - top) * count_of(f).astype(F32)
        scores[128 * f : 128 * f + 128] = e
        total = total + jnp.sum(e, axis=0, keepdims=True)
        et[:, 128 * f : 128 * f + 128] = e.T.astype(BF16)
    pet[...] = pe.T.astype(BF16)

    filler = jnp.zeros((5, PLANE), F32)
    whole = jnp.concatenate([top, total, pos, filler], axis=0)
    for n, axis in enumerate("xyz"):
        g = at[axis]
        stats[n, g] = whole
        for delta in (1, 2, 3):
            k = n * 4 + delta
            pending.append(send(
                stats.at[n, g], stats.at[n, g], st_send.at[k],
                st_recv.at[k], peer(axis, delta),
            ))
        for delta in (1, 2, 3):
            arrived(stats.at[n, lax.rem(g + 4 - delta, 4)], st_recv.at[n * 4 + delta])
        parts = [stats[n, i] for i in range(4)]
        best = parts[0][0:1]
        for i in range(1, 4):
            best = jnp.maximum(best, parts[i][0:1])
        summed = jnp.zeros_like(best)
        positive = jnp.zeros_like(best)
        for i in range(4):
            summed = summed + parts[i][1:2] * jnp.exp(parts[i][0:1] - best)
            positive = positive + parts[i][2:3]
        whole = jnp.concatenate([best, summed, positive, filler], axis=0)
    log_total = best + jnp.log(summed)
    loss_own[...] = jnp.broadcast_to(jnp.sum(log_total - positive, axis=1, keepdims=True), (8, 128))
    loss_copy = send(loss_own, loss_sib, loss_send, loss_recv, sib)
    factor = jnp.exp(top - log_total) / BATCH

    wp = (pscores[...] * factor - jnp.where(same, 1.0 / BATCH, 0.0)).astype(BF16)
    wx[0:ROWS] = (scores[ROWS : 2 * ROWS] * factor).astype(BF16)
    wx[ROWS : ROWS + 16] = wp
    w_copy = send(wx, wd.at[:, PLANE : 2 * PLANE], w_send, w_recv, sib)
    wd[0:ROWS, 0:PLANE] = (scores[0:ROWS] * factor).astype(BF16)
    wd[ROWS : ROWS + 16, 0:PLANE] = wp

    wide = jnp.broadcast_to(factor * SCALE, (128, PLANE))
    for x in range(4):
        fcol[128 * x : 128 * x + 128] = wide[:, 128 * x : 128 * x + 128].T

    ds = (d0, d1, d2)
    own_row = pl.multiple_of(jnp.where(in_plane, first, 0), 16)

    def back(i, _):
        z, y = i // 4, lax.rem(i, 4)
        cols = pl.ds(pl.multiple_of(i * 256, 256), 256)
        right = pool[:, cols]
        pright = pas[:, cols]
        own_piece = jnp.where(in_plane, pright.astype(F32) * (SCALE / BATCH), 0.0)
        for x in range(4):
            rows = slice(128 * x, 128 * x + 128)
            acc = jnp.dot(et[rows], right, preferred_element_type=F32)
            acc = acc + jnp.dot(pet[rows], pright, preferred_element_type=F32)
            f = fcol[rows]
            acc = acc * jnp.concatenate([f, f], axis=1)
            placed = jnp.concatenate([own_piece] * 8, axis=0)
            r = lax.broadcasted_iota(jnp.int32, (128, 256), 0) + 128 * x
            hit = jnp.logical_and(r >= own_row, r < own_row + 16)
            acc = acc - jnp.where(hit, placed, 0.0)
            acc = acc.astype(BF16)
            where = {"x": x, "y": y, "z": z}
            for part in range(3):
                aa, bb, cc = ORDERS[part]
                o = PART_OFF[part]
                ds[part][where[cc], where[bb], where[aa]] = acc[o : o + RS_ROWS[part]]
        return 0

    lax.fori_loop(0, 16, back, 0)

    bufs = (
        (((h0a, h0b, f0a, f0b), (h0c, h0d, f0c, f0d), (i0a, i0b, g0a, g0b))),
        (((h1a, h1b, f1a, f1b), (h1c, h1d, f1c, f1d), (i1a, i1b, g1a, g1b))),
        (((h2a, h2b, f2a, f2b), (h2c, h2d, f2c, f2d), (i2a, i2b, g2a, g2b))),
    )

    def add_into(dst, srcs, lead):
        if len(lead) == 0:
            total = dst[...].astype(F32)
            for src in srcs:
                total = total + src[...].astype(F32)
            dst[...] = total.astype(BF16)
            return
        count = 1
        for n in lead:
            count *= n

        def body(i, _):
            index = (i,) if len(lead) == 1 else (i // lead[1], lax.rem(i, lead[1]))
            total = dst[index].astype(F32)
            for src in srcs:
                total = total + src[index].astype(F32)
            dst[index] = total.astype(BF16)
            return 0

        lax.fori_loop(0, count, body, 0)

    def rs_views(part, phase):
        buf = ds[part]
        c, b, a = slot(part)
        if phase == 0:
            return lambda g: buf.at[g], lambda g, h: buf.at[g, 2 * h : 2 * h + 2], (2, 4), (4, 4)
        if phase == 1:
            return lambda g: buf.at[c, g], lambda g, h: buf.at[c, g, 2 * h : 2 * h + 2], (2,), (4,)
        return lambda g: buf.at[c, b, g], lambda g, h: buf.at[c, b, g, :, 128 * h : 128 * h + 128], (), ()

    def rs_phase(phase):
        views = []
        for part in range(3):
            axis = ORDERS[part][2 - phase]
            block, half, half_lead, lead = rs_views(part, phase)
            hl, hr, fl, fr = bufs[part][phase]
            g = at[axis]
            k = (part * 3 + phase) * 4
            right, left = peer(axis, 1), peer(axis, 3)
            far = lax.rem(g + 2, 4)
            pending.append(send(half(far, 0), hl, rs_send.at[k], rs_recv.at[k], right))
            pending.append(send(half(far, 1), hr, rs_send.at[k + 1], rs_recv.at[k + 1], left))
            views.append((block, half, half_lead, lead, g, k, right, left, hl, hr, fl, fr))
        for block, half, half_lead, lead, g, k, right, left, hl, hr, fl, fr in views:
            before, after = lax.rem(g + 3, 4), lax.rem(g + 1, 4)
            arrived(hl, rs_recv.at[k])
            add_into(half(after, 0), (hl,), half_lead)
            pending.append(send(block(after), fl, rs_send.at[k + 2], rs_recv.at[k + 2], right))
            arrived(hr, rs_recv.at[k + 1])
            add_into(half(before, 1), (hr,), half_lead)
            pending.append(send(block(before), fr, rs_send.at[k + 3], rs_recv.at[k + 3], left))
        return views

    def rs_finish(views):
        for block, half, half_lead, lead, g, k, right, left, hl, hr, fl, fr in views:
            arrived(fl, rs_recv.at[k + 2])
            arrived(fr, rs_recv.at[k + 3])
            add_into(block(g), (fl, fr), lead)

    views = rs_phase(0)

    q_copy.wait_recv()
    w_copy.wait_recv()

    def pool_grad(i, _):
        cols = pl.ds(pl.multiple_of(i * 512, 512), 512)
        acc = jnp.dot(wd[...], queries[:, cols], preferred_element_type=F32) * SCALE
        out[:, cols] = acc[0:ROWS].astype(BF16)
        gp_tx[:, cols] = acc[ROWS : ROWS + 16].astype(BF16)
        pltpu.make_async_copy(out.at[:, cols], gpool_ref.at[:, cols], out_sem).start()
        return 0

    lax.fori_loop(0, 8, pool_grad, 0)

    plane_of = zy // 8
    for t in range(8):
        there = core * 8 + t
        target = (at["x"] * 2 + plane_of, there)
        me = jnp.logical_and(there == zy, plane_of == core)
        src = gp_tx.at[:, pl.ds(pl.multiple_of(there * 256, 256), 256)]
        place = lax.rem(zy, 8)

        @pl.when(me)
        def _():
            pltpu.make_async_copy(src, gp_rx.at[place], gp_recv.at[place]).start()

        @pl.when(jnp.logical_not(me))
        def _():
            send(src, gp_rx.at[place], gp_send.at[t], gp_recv.at[place], target)

    rs_finish(views)
    rs_finish(rs_phase(1))
    rs_finish(rs_phase(2))

    for part in range(3):
        c, b, a = slot(part)
        o = PART_OFF[part]
        gq_ref[o : o + RS_ROWS[part]] = ds[part][c, b, a]
    for i in range(8):
        arrived(gp_rx.at[i], gp_recv.at[i])
        gp_ref[16 * i : 16 * i + 16] = gp_rx[i]
    loss_copy.wait_recv()
    loss_ref[...] = (loss_own[...] + loss_sib[...]) / BATCH

    for copy in pending:
        copy.wait_send()
    for copy in (pool_copy, q_copy, w_copy, loss_copy):
        copy.wait_send()
    for t in range(8):
        for other in range(2):
            chip = core * 8 + t
            me = jnp.logical_and(chip == zy, core == other)

            @pl.when(jnp.logical_not(me))
            def _():
                arrived(p_ref.at[16 * t : 16 * t + 16], pas_send.at[t * 2 + other])

        me = jnp.logical_and(core * 8 + t == zy, plane_of == core)

        @pl.when(jnp.logical_not(me))
        def _():
            arrived(gp_rx.at[0], gp_send.at[t])

    pltpu.make_async_copy(out, gpool_ref, out_sem).wait()


def body(queries, passages, pool_rows, negatives):
    names = jnp.pad(negatives, ((0, 0), (0, 256 - NEGS)))
    vmem = pl.BlockSpec(memory_space=pltpu.VMEM)
    hbm = pl.BlockSpec(memory_space=pl.ANY)
    dma = pltpu.SemaphoreType.DMA
    rs = []
    for rows in RS_ROWS:
        rs += [pltpu.VMEM((2, 4, rows, 256), BF16)] * 2
        rs += [pltpu.VMEM((2, rows, 256), BF16)] * 2
        rs += [pltpu.VMEM((4, 4, rows, 256), BF16)] * 2
        rs += [pltpu.VMEM((4, rows, 256), BF16)] * 2
        rs += [pltpu.VMEM((rows, 128), BF16)] * 2
        rs += [pltpu.VMEM((rows, 256), BF16)] * 2
    loss, gq, gp, gpool = pl.pallas_call(
        kernel,
        out_shape=(
            jax.ShapeDtypeStruct((8, 128), F32),
            jax.ShapeDtypeStruct((128, 256), BF16),
            jax.ShapeDtypeStruct((128, 256), BF16),
            jax.ShapeDtypeStruct((ROWS, D), BF16),
        ),
        in_specs=[vmem, vmem, hbm, vmem],
        out_specs=(vmem, vmem, vmem, hbm),
        scratch_shapes=[
            *[pltpu.VMEM((4, 4, 4, AG_ROWS, 256), BF16)] * 3,
            pltpu.VMEM((2 * ROWS, D), BF16),
            pltpu.VMEM((2 * PLANE, D), BF16),
            pltpu.VMEM((16, 16, 256), BF16),
            pltpu.VMEM((16, D), BF16),
            pltpu.VMEM((2 * ROWS, PLANE), F32),
            pltpu.VMEM((16, PLANE), F32),
            pltpu.VMEM((128, PLANE), jnp.int32),
            pltpu.VMEM((PLANE, 2 * ROWS), BF16),
            pltpu.VMEM((PLANE, 16), BF16),
            pltpu.VMEM((ROWS + 16, 2 * PLANE), BF16),
            pltpu.VMEM((ROWS + 16, PLANE), BF16),
            pltpu.VMEM((PLANE, 128), F32),
            pltpu.VMEM((3, 4, 8, PLANE), F32),
            pltpu.VMEM((8, 128), F32),
            pltpu.VMEM((8, 128), F32),
            pltpu.VMEM((16, D), BF16),
            pltpu.VMEM((8, 16, 256), BF16),
            pltpu.VMEM((ROWS, D), BF16),
            *[pltpu.VMEM((4, 4, 4, rows, 256), BF16) for rows in RS_ROWS],
            *rs,
            dma, dma, dma, dma((36,)), dma((36,)), dma((16,)), dma((16,)), dma, dma,
            dma((12,)), dma((12,)), dma, dma, dma((36,)), dma((36,)), dma((8,)), dma((8,)), dma, dma, dma,
        ],
        compiler_params=pltpu.CompilerParams(
            collective_id=0, has_side_effects=True, vmem_limit_bytes=60 * 1024 * 1024
        ),
    )(queries, passages, pool_rows, names)
    return loss[0, 0], gq, gp, gpool


def solution(mesh):
    placed = (P("dp", "mp"), P("dp", "mp"), P(("dp", "mp"), None), P(("dp", "mp"), None))
    return jax.shard_map(
        body,
        mesh=mesh,
        in_specs=placed,
        out_specs=(P(), P("dp", "mp"), P("dp", "mp"), P(("dp", "mp"), None)),
        check_vma=False,
    )
```

time: 503 us -> 112 us (0.22)
  the two profiles are of different devices: /device:TPU:1 before, /device:TPU:0 now
where the time goes in v1:
time: 112 us; the launch traced here: 111 us
  Pallas kernels  101 us (90%)
  local copies, waits for them, and re-layouts  10.1 us (9%)
    pallas_call x1, Pallas kernels, body(): pl.pallas_call(kernel, out_shape=(jax.ShapeDtypeStruct((8, 128), F32), ja...  101 us
    unnamed x3, local copies, waits for them, and re-layouts  7.64 us

profile of v1, /device:TPU:0, one launch (start us, length us, event | category | flops | bytes accessed | tf_op | source)
XLA Modules:
  0.0 111.5 jit_solution(5513776923646290611)
XLA Ops:
  0.6 1.3 %pad.4.neg_ref = s32[8,256]{1,0:T(8,128)} pad(s32[8,31]{1,0:T(8,128)} %param.7, s32[]{:T(128)} %constant.0.clone.1), padding=0_0x0_225 | pad | bytes 9188 | tf_op jit(solution)/shard_map/jit(_pad)/pad | solution.py:423
  1.9 100.7 %shard_map.75 = (f32[8,128]{1,0:T(8,128)}, bf16[128,256]{1,0:T(8,128)(2,1)}, bf16[128,256]{1,0:T(8,128)(2,1)}, bf16[512,4096]{1,0:T(8,128)(2,1)}) custom-call(bf16[128,256]{1,0:T(8,128)(2,1)} %q_ref.1, bf16[128,256]{1,0:T(8,128)(2,1)} %p_ref.1, bf16[512,4096]{1,0:T(8,128)(2,1)} %pool_ref.1, s32[8,256]{1,0:T(8,128)} %pad.4.neg_ref), custom_call_target="tpu_custom_call" | custom-call | tf_op jit(solution)/shard_map/pallas_call | solution.py:435
  102.6 1.2 %slice.3 = f32[1,1]{1,0:T(1,128)} slice(f32[8,128]{1,0:T(8,128)} %get-tuple-element.8), slice={[0:1], [0:1]} | slice | bytes 8 | tf_op jit(solution)/shard_map/slice | solution.py:474
  103.8 1.5 %copy.11 = bf16[128,256]{1,0:T(8,128)(2,1)} copy(bf16[128,256]{1,0:T(8,128)(2,1)} %get-tuple-element.17) | data formatting | bytes 131072
  105.3 1.5 %copy.12 = bf16[128,256]{1,0:T(8,128)(2,1)} copy(bf16[128,256]{1,0:T(8,128)(2,1)} %get-tuple-element.18) | data formatting | bytes 131072
  106.8 4.7 %copy.13 = bf16[512,4096]{1,0:T(8,128)(2,1)} copy(bf16[512,4096]{1,0:T(8,128)(2,1)} %get-tuple-element.19) | data formatting | bytes 8388608

commit v2 on v1

v2 whole, which is shorter than its diff:
```python
import jax
import jax.numpy as jnp
from jax import lax
from jax.experimental import pallas as pl
from jax.experimental.pallas import tpu as pltpu
from jax.sharding import PartitionSpec as P

MESH = pl.DeviceIdType.MESH
F32 = jnp.float32
BF16 = jnp.bfloat16

D = 4096
NEGS = 31
BATCH = 1024
ROWS = 512
PLANE = 512
SCALE = 1.0 / 64.0
ORDERS = ("xyz", "yzx", "zxy")
PART_OFF = (0, 48, 96)
AG_ROWS = 48
RS_ROWS = (48, 48, 32)
LOW = -1e30


def kernel(
    q_ref, p_ref, pool_ref, neg_ref,
    loss_ref, gq_ref, gp_ref, gpool_ref,
    ag0, ag1, ag2, pool, queries, pas_rx, pas, scores, pscores, names, et, pet, wd, wx, cols_of,
    stats, loss_own, loss_sib, gp_tx, gp_rx, out,
    d0, d1, d2, hl0, hl1, hl2, hr0, hr1, hr2, fl0, fl1, fl2, fr0, fr1, fr2, r10, r11, r12, r20, r21, r22,
    local_sem, pool_send, pool_recv, ag_send, ag_recv, pas_send, pas_recv, q_send, q_recv,
    st_send, st_recv, w_send, w_recv, rs_send, rs_recv, gp_send, gp_recv, loss_send, loss_recv, out_sem,
):
    dp = lax.axis_index("dp")
    mp = lax.axis_index("mp")
    core = lax.rem(dp, 2)
    at = {"x": dp // 2, "y": lax.rem(mp, 4), "z": mp // 4}
    zy = mp
    sib = (at["x"] * 2 + 1 - core, mp)

    def peer(axis, delta):
        there = dict(at)
        there[axis] = lax.rem(at[axis] + delta, 4)
        return (there["x"] * 2 + core, there["z"] * 4 + there["y"])

    def send(src, dst, send_sem, recv_sem, device):
        copy = pltpu.make_async_remote_copy(
            src_ref=src, dst_ref=dst, send_sem=send_sem, recv_sem=recv_sem,
            device_id=device, device_id_type=MESH,
        )
        copy.start()
        return copy

    def arrived(ref, sem):
        pltpu.make_async_copy(ref, ref, sem).wait()

    barrier = pltpu.get_barrier_semaphore()
    for axis in "xyz":
        for delta in (1, 2, 3):
            pl.semaphore_signal(barrier, inc=1, device_id=peer(axis, delta), device_id_type=MESH)
    pl.semaphore_signal(barrier, inc=1, device_id=sib, device_id_type=MESH)

    pending = []
    own_pool = pltpu.make_async_copy(pool_ref, pool.at[0:ROWS], local_sem)
    own_pool.start()

    ags = (ag0, ag1, ag2)

    def slot(part):
        a, b, c = ORDERS[part]
        return at[c], at[b], at[a]

    ids = neg_ref[...]
    high = (ids >> 8).astype(F32)
    low = (ids & 255).astype(F32)
    tile = jnp.concatenate([high, low], axis=0)
    tile = jnp.concatenate([tile, jnp.zeros((16, 128 - NEGS), F32)], axis=1).astype(BF16)
    for s in range(2):
        cols = slice(128 * s, 128 * s + 128)
        for part in range(3):
            c, b, a = slot(part)
            o = PART_OFF[part]
            ags[part][s, c, b, a, 0 : RS_ROWS[part]] = q_ref[o : o + RS_ROWS[part], cols]
        ag2[s, c, b, a, 32:48] = tile
    pl.semaphore_wait(barrier, 10)

    for part in range(3):
        c, b, a = slot(part)
        own = ags[part].at[:, c, b, a]
        for delta in (1, 2, 3):
            k = part * 22 + delta - 1
            pending.append(send(own, own, ag_send.at[k], ag_recv.at[k], peer(ORDERS[part][0], delta)))
    pool_copy = send(pool_ref, pool.at[ROWS : 2 * ROWS], pool_send, pool_recv, sib)

    def third(part, j, view, k):
        axis = ORDERS[part][2]
        pending.append(send(view, view, ag_send.at[k], ag_recv.at[k], peer(axis, 1)))
        pending.append(send(view, view, ag_send.at[k + 1], ag_recv.at[k + 1], peer(axis, 3)))

    for part in range(3):
        c, b, a = slot(part)
        buf = ags[part]
        for delta in (1, 2, 3):
            arrived(buf.at[:, c, b, lax.rem(a + 4 - delta, 4)], ag_recv.at[part * 22 + delta - 1])
        line = buf.at[:, c, b]
        for delta in (1, 2, 3):
            k = part * 22 + 3 + delta - 1
            pending.append(send(line, line, ag_send.at[k], ag_recv.at[k], peer(ORDERS[part][1], delta)))
        third(part, 0, buf.at[0, c, b], part * 22 + 6)
    for part in range(3):
        c, b, a = slot(part)
        buf = ags[part]
        for delta in (1, 2, 3):
            arrived(buf.at[:, c, lax.rem(b + 4 - delta, 4)], ag_recv.at[part * 22 + 3 + delta - 1])
        for j in (1, 2, 3):
            third(part, j, buf.at[0, c, lax.rem(b + j, 4)], part * 22 + 6 + 2 * j)
    for part in range(3):
        c, b, a = slot(part)
        third(part, 0, ags[part].at[1, c], part * 22 + 18)

    for t in range(8):
        for other in range(2):
            chip = core * 8 + t
            target = (at["x"] * 2 + other, chip)
            me = jnp.logical_and(chip == zy, core == other)
            src = p_ref.at[16 * t : 16 * t + 16]
            dst = pas_rx.at[zy]
            k = t * 2 + other

            @pl.when(me)
            def _():
                pltpu.make_async_copy(src, dst, pas_recv.at[zy]).start()

            @pl.when(jnp.logical_not(me))
            def _():
                send(src, dst, pas_send.at[k], pas_recv.at[zy], target)

    for part in range(3):
        c, b, a = slot(part)
        buf = ags[part]
        axis = ORDERS[part][2]
        before, after = lax.rem(c + 3, 4), lax.rem(c + 1, 4)
        for j in range(4):
            bb = lax.rem(b + j, 4)
            k = part * 22 + 6 + 2 * j
            kf = part * 22 + 14 + j
            arrived(buf.at[0, before, bb], ag_recv.at[k])
            arrived(buf.at[0, after, bb], ag_recv.at[k + 1])
            view = buf.at[0, before if j < 2 else after, bb]
            pending.append(send(view, view, ag_send.at[kf], ag_recv.at[kf], peer(axis, 1 if j < 2 else 3)))
    for part in range(3):
        c, b, a = slot(part)
        buf = ags[part]
        axis = ORDERS[part][2]
        before, after = lax.rem(c + 3, 4), lax.rem(c + 1, 4)
        k = part * 22 + 18
        arrived(buf.at[1, before], ag_recv.at[k])
        view = buf.at[1, before, 0:2]
        pending.append(send(view, view, ag_send.at[k + 2], ag_recv.at[k + 2], peer(axis, 1)))
        arrived(buf.at[1, after], ag_recv.at[k + 1])
        view = buf.at[1, after, 2:4]
        pending.append(send(view, view, ag_send.at[k + 3], ag_recv.at[k + 3], peer(axis, 3)))

    contract = (((1,), (1,)), ((), ()))

    def assemble(s):
        def one(i, _):
            z, y = i // 4, lax.rem(i, 4)
            cols = pl.ds(pl.multiple_of(i * 256 + 128 * s, 128), 128)
            for x in range(4):
                where = {"x": x, "y": y, "z": z}
                for part in range(3):
                    aa, bb, cc = ORDERS[part]
                    rows = RS_ROWS[part]
                    start = x * 128 + PART_OFF[part]
                    queries[start : start + rows, cols] = ags[part][s, where[cc], where[bb], where[aa], 0:rows]
            return 0

        lax.fori_loop(0, 16, one, 0)

    def halves(ref, rows, first, count, s):
        return jnp.concatenate(
            [
                ref[rows, pl.ds(pl.multiple_of((first + j) * 256 + 128 * s, 128), 128)]
                for j in range(count)
            ],
            axis=1,
        )

    everything = slice(None)
    plane = slice(0, PLANE)

    def score(s):
        def one(i, _):
            left = halves(pool, everything, 8 * i, 8, s)
            right = halves(queries, plane, 8 * i, 8, s)
            scores[...] += lax.dot_general(left, right, contract, preferred_element_type=F32)
            return 0

        lax.fori_loop(0, 2, one, 0)

    scores[...] = jnp.zeros_like(scores)
    for part in range(3):
        c, b, a = slot(part)
        far = lax.rem(c + 2, 4)
        for j in range(4):
            arrived(ags[part].at[0, far, lax.rem(b + j, 4)], ag_recv.at[part * 22 + 14 + j])
    assemble(0)

    mine = dp * 16 + mp
    theirs = (at["x"] * 2 + 1 - core) * 16 + mp
    sub = lax.broadcasted_iota(jnp.int32, (128, 128), 0)
    for x in range(4):
        pieces = []
        for i in range(16):
            where = {"x": x, "y": i % 4, "z": i // 4}
            aa, bb, cc = ORDERS[2]
            tile = ag2[0, where[cc], where[bb], where[aa], 32:48].astype(F32)
            pieces.append(tile[0:8] * 256.0 + tile[8:16])
        named = jnp.concatenate(pieces, axis=0).T[0:32].astype(jnp.int32)
        owner = named >> 9
        field = ((named >> 7) & 3) * 4
        bit = jnp.where(
            owner == mine, jnp.left_shift(1, field),
            jnp.where(owner == theirs, jnp.left_shift(1, field + 16), 0),
        )
        hi = named & 127
        packed = jnp.zeros((128, 128), jnp.int32)
        for k in range(NEGS):
            packed = packed + jnp.where(sub == hi[k : k + 1], bit[k : k + 1], 0)
        names[:, 128 * x : 128 * x + 128] = packed

    own_pool.wait()
    pool_copy.wait_recv()
    score(0)
    for i in range(16):
        arrived(pas_rx.at[i], pas_recv.at[i])
        pas[:, 256 * i : 256 * i + 256] = pas_rx[i]

    for part in range(3):
        c, b, a = slot(part)
        far = lax.rem(c + 2, 4)
        arrived(ags[part].at[1, far, 0:2], ag_recv.at[part * 22 + 20])
        arrived(ags[part].at[1, far, 2:4], ag_recv.at[part * 22 + 21])
    assemble(1)
    q_copy = send(queries.at[0:PLANE], queries.at[PLANE : 2 * PLANE], q_send, q_recv, sib)
    score(1)
    ps = lax.dot_general(pas[...], queries[0:PLANE, :], contract, preferred_element_type=F32) * SCALE

    lane = lax.broadcasted_iota(jnp.int32, (16, PLANE), 1)
    psub = lax.broadcasted_iota(jnp.int32, (16, PLANE), 0)
    in_plane = core == zy // 8
    first = jnp.where(in_plane, at["x"] * 128 + lax.rem(zy, 8) * 16, -1024)
    same = lane == first + psub
    pos = jnp.sum(jnp.where(same, ps, 0.0), axis=0, keepdims=True)

    def count_of(f):
        return (names[...] >> (4 * f)) & 15

    top = jnp.max(ps, axis=0, keepdims=True)
    for f in range(8):
        s = jnp.where(count_of(f) > 0, scores[128 * f : 128 * f + 128] * SCALE, LOW)
        scores[128 * f : 128 * f + 128] = s
        top = jnp.maximum(top, jnp.max(s, axis=0, keepdims=True))
    pe = jnp.exp(ps - top)
    pscores[...] = pe
    total = jnp.sum(pe, axis=0, keepdims=True)
    for f in range(8):
        e = jnp.exp(scores[128 * f : 128 * f + 128] - top) * count_of(f).astype(F32)
        scores[128 * f : 128 * f + 128] = e
        total = total + jnp.sum(e, axis=0, keepdims=True)
        et[:, 128 * f : 128 * f + 128] = e.T.astype(BF16)
    pet[...] = pe.T.astype(BF16)

    filler = jnp.zeros((5, PLANE), F32)
    within = lax.rem(lax.broadcasted_iota(jnp.int32, (1, PLANE), 1), 128)

    def by_part(values):
        return jnp.where(within < 48, values[0], jnp.where(within < 96, values[1], values[2]))

    def stats_send(n, values):
        tile = jnp.concatenate(list(values) + [filler], axis=0)
        for i, axis in enumerate("xyz"):
            g = at[axis]
            stats[n, i, g] = tile
            for delta in (1, 2, 3):
                k = n * 9 + i * 3 + delta - 1
                ref = stats.at[n, i, g]
                pending.append(send(ref, ref, st_send.at[k], st_recv.at[k], peer(axis, delta)))

    def stats_meet(n):
        sums = {}
        for i, axis in enumerate("xyz"):
            g = at[axis]
            for delta in (1, 2, 3):
                arrived(stats.at[n, i, lax.rem(g + 4 - delta, 4)], st_recv.at[n * 9 + i * 3 + delta - 1])
            parts = [stats[n, i, j] for j in range(4)]
            best = parts[0][0:1]
            for j in range(1, 4):
                best = jnp.maximum(best, parts[j][0:1])
            summed = jnp.zeros_like(best)
            positive = jnp.zeros_like(best)
            for j in range(4):
                summed = summed + parts[j][1:2] * jnp.exp(parts[j][0:1] - best)
                positive = positive + parts[j][2:3]
            sums[axis] = (best, summed, positive)
        return tuple(by_part([sums[ORDERS[part][2 - n]][v] for part in range(3)]) for v in range(3))

    def place_column(index, row):
        wide = jnp.broadcast_to(row, (128, PLANE))
        for x in range(4):
            cols_of[index, 128 * x : 128 * x + 128] = wide[:, 128 * x : 128 * x + 128].T

    stats_send(0, (top, total, pos))

    ds = (d0, d1, d2)

    def back(s):
        def one(i, _):
            right = halves(pool, everything, 2 * i, 2, s)
            pright = halves(pas, everything, 2 * i, 2, s)
            acc = jnp.dot(et[...], right, preferred_element_type=F32)
            acc = (acc + jnp.dot(pet[...], pright, preferred_element_type=F32)).astype(BF16)
            for j in range(2):
                z, y = (2 * i + j) // 4, lax.rem(2 * i + j, 4)
                for x in range(4):
                    where = {"x": x, "y": y, "z": z}
                    for part in range(3):
                        aa, bb, cc = ORDERS[part]
                        o = x * 128 + PART_OFF[part]
                        ds[part][s, where[cc], where[bb], where[aa]] = acc[o : o + RS_ROWS[part], 128 * j : 128 * j + 128]
            return 0

        lax.fori_loop(0, 8, one, 0)

    hls, hrs, fls, frs = (hl0, hl1, hl2), (hr0, hr1, hr2), (fl0, fl1, fl2), (fr0, fr1, fr2)
    r1s, r2s = (r10, r11, r12), (r20, r21, r22)

    def scatter_key(part, s):
        return (part * 2 + s) * 12

    def scatter_start(s):
        for part in range(3):
            c, b, a = slot(part)
            axis = ORDERS[part][2]
            k = scatter_key(part, s)
            d = ds[part]
            far, before, after = lax.rem(c + 2, 4), lax.rem(c + 3, 4), lax.rem(c + 1, 4)
            right, left = peer(axis, 1), peer(axis, 3)
            pending.append(send(d.at[s, far, 0:2], hls[part].at[s], rs_send.at[k], rs_recv.at[k], right))
            pending.append(send(d.at[s, far, 2:4], hrs[part].at[s], rs_send.at[k + 1], rs_recv.at[k + 1], left))
            pending.append(send(d.at[s, after, 2:4], fls[part].at[s, 2:4], rs_send.at[k + 2], rs_recv.at[k + 2], right))
            pending.append(send(d.at[s, before, 0:2], frs[part].at[s, 0:2], rs_send.at[k + 3], rs_recv.at[k + 3], left))

    def factor_rows(part, index, c, b, a):
        x = dict(zip(ORDERS[part], (a, b, c)))["x"]
        return cols_of[index, pl.ds(pl.multiple_of(x * 128 + PART_OFF[part], 16), RS_ROWS[part])]

    def scatter_forward(s):
        for part in range(3):
            c, b, a = slot(part)
            axis = ORDERS[part][2]
            k = scatter_key(part, s)
            d, hl, hr = ds[part], hls[part], hrs[part]
            before, after = lax.rem(c + 3, 4), lax.rem(c + 1, 4)

            def add(i, _, block, base, rx, column):
                bb, aa = i // 4, lax.rem(i, 4)
                own = d[s, block, base + bb, aa].astype(F32) * factor_rows(part, 0, block, base + bb, aa)
                other = rx[s, bb, aa].astype(F32) * factor_rows(part, column, block, base + bb, aa)
                d[s, block, base + bb, aa] = (own + other).astype(BF16)
                return 0

            arrived(hl.at[s], rs_recv.at[k])
            lax.fori_loop(0, 8, lambda i, t: add(i, t, after, 0, hl, 1), 0)
            pending.append(send(
                d.at[s, after, 0:2], fls[part].at[s, 0:2], rs_send.at[k + 4], rs_recv.at[k + 4], peer(axis, 1)
            ))
            arrived(hr.at[s], rs_recv.at[k + 1])
            lax.fori_loop(0, 8, lambda i, t: add(i, t, before, 2, hr, 2), 0)
            pending.append(send(
                d.at[s, before, 2:4], frs[part].at[s, 2:4], rs_send.at[k + 5], rs_recv.at[k + 5], peer(axis, 3)
            ))

    def scatter_second(s):
        for part in range(3):
            c, b, a = slot(part)
            k = scatter_key(part, s)
            d, fl, fr = ds[part], fls[part], frs[part]
            arrived(fl.at[s, 2:4], rs_recv.at[k + 2])
            arrived(fr.at[s, 0:2], rs_recv.at[k + 3])
            arrived(fl.at[s, 0:2], rs_recv.at[k + 4])
            arrived(fr.at[s, 2:4], rs_recv.at[k + 5])

            def low_half(i, _):
                bb, aa = i // 4, lax.rem(i, 4)
                total = d[s, c, bb, aa].astype(F32) * factor_rows(part, 0, c, bb, aa)
                total = total + fr[s, bb, aa].astype(F32) * factor_rows(part, 2, c, bb, aa) + fl[s, bb, aa].astype(F32)
                d[s, c, bb, aa] = (total * factor_rows(part, 3, c, bb, aa)).astype(BF16)
                return 0

            def high_half(i, _):
                bb, aa = i // 4 + 2, lax.rem(i, 4)
                total = d[s, c, bb, aa].astype(F32) * factor_rows(part, 0, c, bb, aa)
                total = total + fl[s, bb, aa].astype(F32) * factor_rows(part, 1, c, bb, aa) + fr[s, bb, aa].astype(F32)
                d[s, c, bb, aa] = (total * factor_rows(part, 3, c, bb, aa)).astype(BF16)
                return 0

            lax.fori_loop(0, 8, low_half, 0)
            lax.fori_loop(0, 8, high_half, 0)
            for delta in (1, 2, 3):
                pending.append(send(
                    d.at[s, c, lax.rem(b + delta, 4)], r1s[part].at[s, delta - 1],
                    rs_send.at[k + 5 + delta], rs_recv.at[k + 5 + delta], peer(ORDERS[part][1], delta),
                ))

    def scatter_third(s):
        for part in range(3):
            c, b, a = slot(part)
            k = scatter_key(part, s)
            d, r1 = ds[part], r1s[part]
            for delta in (1, 2, 3):
                arrived(r1.at[s, delta - 1], rs_recv.at[k + 5 + delta])
            for aa in range(4):
                total = d[s, c, b, aa].astype(F32)
                for j in range(3):
                    total = total + r1[s, j, aa].astype(F32)
                d[s, c, b, aa] = (total * factor_rows(part, 4, c, b, aa)).astype(BF16)
            for delta in (1, 2, 3):
                pending.append(send(
                    d.at[s, c, b, lax.rem(a + delta, 4)], r2s[part].at[s, delta - 1],
                    rs_send.at[k + 8 + delta], rs_recv.at[k + 8 + delta], peer(ORDERS[part][0], delta),
                ))

    def scatter_end(s):
        for part in range(3):
            c, b, a = slot(part)
            k = scatter_key(part, s)
            d, r2 = ds[part], r2s[part]
            total = d[s, c, b, a].astype(F32)
            for delta in (1, 2, 3):
                arrived(r2.at[s, delta - 1], rs_recv.at[k + 8 + delta])
                total = total + r2[s, delta - 1].astype(F32)
            rows = slice(PART_OFF[part], PART_OFF[part] + RS_ROWS[part])
            cols = slice(128 * s, 128 * s + 128)
            total = total * factor_rows(part, 5, c, b, a) - p_ref[rows, cols].astype(F32) * (SCALE / BATCH)
            gq_ref[rows, cols] = total.astype(BF16)

    back(0)
    scatter_start(0)
    back(1)
    scatter_start(1)

    best1, sum1, pos1 = stats_meet(0)
    stats_send(1, (best1, sum1, pos1))
    place_column(0, jnp.exp(top - best1))
    for index, delta in ((1, 3), (2, 1)):
        theirs_top = by_part([
            stats[0, "xyz".index(ORDERS[part][2]), lax.rem(at[ORDERS[part][2]] + delta, 4)][0:1] for part in range(3)
        ])
        place_column(index, jnp.exp(theirs_top - best1))

    scatter_forward(0)
    scatter_forward(1)

    best2, sum2, pos2 = stats_meet(1)
    stats_send(2, (best2, sum2, pos2))
    place_column(3, jnp.exp(best1 - best2))

    scatter_second(0)

    best3, sum3, pos3 = stats_meet(2)
    log_total = best3 + jnp.log(sum3)
    place_column(4, jnp.exp(best2 - best3))
    place_column(5, jnp.exp(best3 - log_total) * (SCALE / BATCH))
    loss_own[...] = jnp.broadcast_to(jnp.sum(log_total - pos3, axis=1, keepdims=True), (8, 128))
    loss_copy = send(loss_own, loss_sib, loss_send, loss_recv, sib)
    factor = jnp.exp(top - log_total) / BATCH

    wp = (pscores[...] * factor - jnp.where(same, 1.0 / BATCH, 0.0)).astype(BF16)
    wx[0:ROWS] = (scores[ROWS : 2 * ROWS] * factor).astype(BF16)
    wx[ROWS : ROWS + 16] = wp
    w_copy = send(wx, wd.at[:, PLANE : 2 * PLANE], w_send, w_recv, sib)
    wd[0:ROWS, 0:PLANE] = (scores[0:ROWS] * factor).astype(BF16)
    wd[ROWS : ROWS + 16, 0:PLANE] = wp

    scatter_second(1)

    q_copy.wait_recv()
    w_copy.wait_recv()

    def pool_grad(i, _):
        cols = pl.ds(pl.multiple_of(i * 512, 512), 512)
        acc = jnp.dot(wd[...], queries[:, cols], preferred_element_type=F32) * SCALE
        out[:, cols] = acc[0:ROWS].astype(BF16)
        gp_tx[:, cols] = acc[ROWS : ROWS + 16].astype(BF16)
        pltpu.make_async_copy(out.at[:, cols], gpool_ref.at[:, cols], out_sem).start()
        return 0

    lax.fori_loop(0, 4, pool_grad, 0)
    scatter_third(0)
    lax.fori_loop(4, 8, pool_grad, 0)
    scatter_third(1)

    plane_of = zy // 8
    for t in range(8):
        there = core * 8 + t
        target = (at["x"] * 2 + plane_of, there)
        me = jnp.logical_and(there == zy, plane_of == core)
        src = gp_tx.at[:, pl.ds(pl.multiple_of(there * 256, 256), 256)]
        place = lax.rem(zy, 8)

        @pl.when(me)
        def _():
            pltpu.make_async_copy(src, gp_rx.at[place], gp_recv.at[place]).start()

        @pl.when(jnp.logical_not(me))
        def _():
            send(src, gp_rx.at[place], gp_send.at[t], gp_recv.at[place], target)

    scatter_end(0)
    scatter_end(1)

    for i in range(8):
        arrived(gp_rx.at[i], gp_recv.at[i])
        gp_ref[16 * i : 16 * i + 16] = gp_rx[i]
    loss_copy.wait_recv()
    loss_ref[...] = (loss_own[...] + loss_sib[...]) / BATCH

    for copy in pending:
        copy.wait_send()
    for copy in (pool_copy, q_copy, w_copy, loss_copy):
        copy.wait_send()
    for t in range(8):
        for other in range(2):
            chip = core * 8 + t
            me = jnp.logical_and(chip == zy, core == other)

            @pl.when(jnp.logical_not(me))
            def _():
                arrived(p_ref.at[16 * t : 16 * t + 16], pas_send.at[t * 2 + other])

        me = jnp.logical_and(core * 8 + t == zy, plane_of == core)

        @pl.when(jnp.logical_not(me))
        def _():
            arrived(gp_rx.at[0], gp_send.at[t])

    pltpu.make_async_copy(out, gpool_ref, out_sem).wait()


def hand_on(loss_in, gq_in, gp_in, gpool_in, loss_out, gq_out, gp_out, gpool_out):
    gpool_out[...] = gpool_in[...]

    @pl.when(pl.program_id(0) == 0)
    def _():
        loss_out[0, 0] = loss_in[0, 0]
        gq_out[...] = gq_in[...]
        gp_out[...] = gp_in[...]


def body(queries, passages, pool_rows, negatives):
    vmem = pl.BlockSpec(memory_space=pltpu.VMEM)
    smem = pl.BlockSpec(memory_space=pltpu.SMEM)
    hbm = pl.BlockSpec(memory_space=pl.ANY)
    dma = pltpu.SemaphoreType.DMA
    pieces = jax.ShapeDtypeStruct((128, 256), BF16)
    rows_out = jax.ShapeDtypeStruct((ROWS, D), BF16)
    loss, gq, gp, gpool = pl.pallas_call(
        kernel,
        out_shape=(jax.ShapeDtypeStruct((8, 128), F32), pieces, pieces, rows_out),
        in_specs=[vmem, vmem, hbm, vmem],
        out_specs=(vmem, vmem, vmem, hbm),
        scratch_shapes=[
            *[pltpu.VMEM((2, 4, 4, 4, AG_ROWS, 128), BF16)] * 3,
            pltpu.VMEM((2 * ROWS, D), BF16),
            pltpu.VMEM((2 * PLANE, D), BF16),
            pltpu.VMEM((16, 16, 256), BF16),
            pltpu.VMEM((16, D), BF16),
            pltpu.VMEM((2 * ROWS, PLANE), F32),
            pltpu.VMEM((16, PLANE), F32),
            pltpu.VMEM((128, PLANE), jnp.int32),
            pltpu.VMEM((PLANE, 2 * ROWS), BF16),
            pltpu.VMEM((PLANE, 16), BF16),
            pltpu.VMEM((ROWS + 16, 2 * PLANE), BF16),
            pltpu.VMEM((ROWS + 16, PLANE), BF16),
            pltpu.VMEM((6, PLANE, 128), F32),
            pltpu.VMEM((3, 3, 4, 8, PLANE), F32),
            pltpu.VMEM((8, 128), F32),
            pltpu.VMEM((8, 128), F32),
            pltpu.VMEM((16, D), BF16),
            pltpu.VMEM((8, 16, 256), BF16),
            pltpu.VMEM((ROWS, D), BF16),
            *[pltpu.VMEM((2, 4, 4, 4, rows, 128), BF16) for rows in RS_ROWS],
            *[pltpu.VMEM((2, 2, 4, rows, 128), BF16) for rows in RS_ROWS],
            *[pltpu.VMEM((2, 2, 4, rows, 128), BF16) for rows in RS_ROWS],
            *[pltpu.VMEM((2, 4, 4, rows, 128), BF16) for rows in RS_ROWS],
            *[pltpu.VMEM((2, 4, 4, rows, 128), BF16) for rows in RS_ROWS],
            *[pltpu.VMEM((2, 3, 4, rows, 128), BF16) for rows in RS_ROWS],
            *[pltpu.VMEM((2, 3, rows, 128), BF16) for rows in RS_ROWS],
            dma, dma, dma, dma((66,)), dma((66,)), dma((16,)), dma((16,)), dma, dma,
            dma((27,)), dma((27,)), dma, dma, dma((72,)), dma((72,)), dma((8,)), dma((8,)), dma, dma, dma,
        ],
        compiler_params=pltpu.CompilerParams(
            collective_id=0, has_side_effects=True, vmem_limit_bytes=60 * 1024 * 1024
        ),
    )(queries, passages, pool_rows, negatives)
    small = pl.BlockSpec((128, 256), lambda i: (0, 0))
    large = pl.BlockSpec((ROWS // 8, D), lambda i: (i, 0))
    loss, gq, gp, gpool = pl.pallas_call(
        hand_on,
        grid=(8,),
        out_shape=(jax.ShapeDtypeStruct((1, 1), F32), pieces, pieces, rows_out),
        in_specs=[smem, small, small, large],
        out_specs=(smem, small, small, large),
        compiler_params=pltpu.CompilerParams(vmem_limit_bytes=60 * 1024 * 1024),
    )(loss, gq, gp, gpool)
    return loss[0, 0], gq, gp, gpool


def solution(mesh):
    placed = (P("dp", "mp"), P("dp", "mp"), P(("dp", "mp"), None), P(("dp", "mp"), None))
    return jax.shard_map(
        body,
        mesh=mesh,
        in_specs=placed,
        out_specs=(P(), P("dp", "mp"), P("dp", "mp"), P(("dp", "mp"), None)),
        check_vma=False,
    )
```

time: 112 us -> 88.6 us (0.79)
  the two profiles are of different devices: /device:TPU:0 before, /device:TPU:1 now
where the time goes in v2:
time: 88.6 us; the launch traced here: 88.3 us
  Pallas kernels  87.7 us (99%)
    pallas_call x1, Pallas kernels, body(): pl.pallas_call(kernel, out_shape=(jax.ShapeDtypeStruct((8, 128), F32), pi...  81 us
    pallas_call x1, Pallas kernels, body(): pl.pallas_call(hand_on, grid=(8,), out_shape=(jax.ShapeDtypeStruct((1, 1)...  6.73 us

profile of v2, /device:TPU:1, one launch (start us, length us, event | category | flops | bytes accessed | tf_op | source)
XLA Modules:
  0.0 88.3 jit_solution(16235497078110651866)
XLA Ops:
  0.6 81.0 %shard_map.75 = (f32[8,128]{1,0:T(8,128)}, bf16[128,256]{1,0:T(8,128)(2,1)}, bf16[128,256]{1,0:T(8,128)(2,1)}, bf16[512,4096]{1,0:T(8,128)(2,1)}) custom-call(bf16[128,256]{1,0:T(8,128)(2,1)} %q_ref.1, bf16[128,256]{1,0:T(8,128)(2,1)} %p_ref.1, bf16[512,4096]{1,0:T(8,128)(2,1)} %pool_ref.1, s32[8,31]{1,0:T(8,128)} %neg_ref.1), custom_call_target="tpu_custom_call" | custom-call | tf_op jit(solution)/shard_map/pallas_call | solution.py:569
  81.6 6.7 %shard_map.76 = (f32[1,1]{1,0:T(1,128)}, bf16[128,256]{1,0:T(8,128)(2,1)}, bf16[128,256]{1,0:T(8,128)(2,1)}, bf16[512,4096]{1,0:T(8,128)(2,1)}) custom-call(f32[8,128]{1,0:T(8,128)} %get-tuple-element.12.loss_in, bf16[128,256]{1,0:T(8,128)(2,1)} %get-tuple-element.13.gq_in, bf16[128,256]{1,0:T(8,128)(2,1)} %get-tuple-element.14.gp_in, ...), custom_call_target="tpu_custom_call" | custom-call | tf_op jit(solution)/shard_map/pallas_call | solution.py:610

commit v3 on v2

v3 whole, which is shorter than its diff:
```python
import jax
import jax.numpy as jnp
from jax import lax
from jax.experimental import pallas as pl
from jax.experimental.pallas import tpu as pltpu
from jax.sharding import PartitionSpec as P

MESH = pl.DeviceIdType.MESH
F32 = jnp.float32
BF16 = jnp.bfloat16

D = 4096
NEGS = 31
BATCH = 1024
ROWS = 512
PLANE = 512
SCALE = 1.0 / 64.0
ORDERS = ("xyz", "yzx", "zxy")
HALF = 256
AG_ROWS = 48
RS_ROWS = (48, 48, 32)
UNITS = (((0, 48, 0, 0),), ((0, 48, 1, 0),), ((48, 16, 0, 0), (48, 16, 1, 16)))
LOW = -1e30


def kernel(
    q_hbm, p_hbm, pool_ref, neg_hbm,
    loss_ref, gq_ref, gp_ref, gpool_ref,
    q_ref, p_ref, neg_ref, in_sem, ag0, ag1, ag2, pool, queries, pas_rx, scores, names, et, pet, wd, wx, cols_of,
    stats, loss_own, loss_sib, gp_tx, gp_rx,
    d0, d1, d2, hl0, hl1, hl2, hr0, hr1, hr2, fl0, fl1, fl2, fr0, fr1, fr2, r10, r11, r12, r20, r21, r22,
    local_sem, pool_send, pool_recv, ag_send, ag_recv, pas_send, pas_recv, q_send, q_recv,
    st_send, st_recv, w_send, w_recv, rs_send, rs_recv, gp_send, gp_recv, loss_send, loss_recv,
):
    dp = lax.axis_index("dp")
    mp = lax.axis_index("mp")
    core = lax.rem(dp, 2)
    at = {"x": dp // 2, "y": lax.rem(mp, 4), "z": mp // 4}
    zy = mp
    sib = (at["x"] * 2 + 1 - core, mp)

    def peer(axis, delta):
        there = dict(at)
        there[axis] = lax.rem(at[axis] + delta, 4)
        return (there["x"] * 2 + core, there["z"] * 4 + there["y"])

    def send(src, dst, send_sem, recv_sem, device):
        copy = pltpu.make_async_remote_copy(
            src_ref=src, dst_ref=dst, send_sem=send_sem, recv_sem=recv_sem,
            device_id=device, device_id_type=MESH,
        )
        copy.start()
        return copy

    def arrived(ref, sem):
        pltpu.make_async_copy(ref, ref, sem).wait()

    barrier = pltpu.get_barrier_semaphore()
    for axis in "xyz":
        for delta in (1, 2, 3):
            pl.semaphore_signal(barrier, inc=1, device_id=peer(axis, delta), device_id_type=MESH)
    pl.semaphore_signal(barrier, inc=1, device_id=sib, device_id_type=MESH)

    pending = []
    inputs = [
        pltpu.make_async_copy(src, dst, in_sem.at[i])
        for i, (src, dst) in enumerate(((q_hbm, q_ref), (neg_hbm, neg_ref), (p_hbm, p_ref)))
    ]
    for copy in inputs:
        copy.start()
    own_pool = pltpu.make_async_copy(pool_ref, pool.at[0:ROWS], local_sem)
    own_pool.start()

    ags = (ag0, ag1, ag2)

    def slot(part):
        a, b, c = ORDERS[part]
        return at[c], at[b], at[a]

    for copy in inputs:
        copy.wait()
    ids = neg_ref[...]
    high = (ids >> 8).astype(F32)
    low = (ids & 255).astype(F32)
    tile = jnp.concatenate([high, low], axis=0)
    tile = jnp.concatenate([tile, jnp.zeros((16, 128 - NEGS), F32)], axis=1).astype(BF16)
    for s in range(2):
        for part in range(3):
            c, b, a = slot(part)
            for row, rows, h, o in UNITS[part]:
                piece = q_ref[64 * s + row : 64 * s + row + rows, 128 * h : 128 * h + 128]
                ags[part][s, c, b, a, o : o + rows] = piece
        c, b, a = slot(2)
        ag2[s, c, b, a, 32:48] = tile
    pl.semaphore_wait(barrier, 10)

    for part in range(3):
        c, b, a = slot(part)
        own = ags[part].at[:, c, b, a]
        for delta in (1, 2, 3):
            k = part * 25 + delta - 1
            pending.append(send(own, own, ag_send.at[k], ag_recv.at[k], peer(ORDERS[part][0], delta)))
    pool_copy = send(pool_ref, pool.at[ROWS : 2 * ROWS], pool_send, pool_recv, sib)

    def third(part, view, k):
        axis = ORDERS[part][2]
        pending.append(send(view, view, ag_send.at[k], ag_recv.at[k], peer(axis, 1)))
        pending.append(send(view, view, ag_send.at[k + 1], ag_recv.at[k + 1], peer(axis, 3)))

    def second(part, s):
        c, b, a = slot(part)
        line = ags[part].at[s, c, b]
        for delta in (1, 2, 3):
            k = part * 25 + 3 + 3 * s + delta - 1
            pending.append(send(line, line, ag_send.at[k], ag_recv.at[k], peer(ORDERS[part][1], delta)))

    def second_arrived(part, s):
        c, b, a = slot(part)
        for delta in (1, 2, 3):
            arrived(ags[part].at[s, c, lax.rem(b + 4 - delta, 4)], ag_recv.at[part * 25 + 3 + 3 * s + delta - 1])

    for part in range(3):
        c, b, a = slot(part)
        buf = ags[part]
        for delta in (1, 2, 3):
            arrived(buf.at[:, c, b, lax.rem(a + 4 - delta, 4)], ag_recv.at[part * 25 + delta - 1])
        second(part, 0)
        third(part, buf.at[0, c, b], part * 25 + 9)
    for part in range(3):
        second(part, 1)
    for part in range(3):
        c, b, a = slot(part)
        buf = ags[part]
        second_arrived(part, 0)
        for j in (1, 2, 3):
            third(part, buf.at[0, c, lax.rem(b + j, 4)], part * 25 + 9 + 2 * j)

    for t in range(8):
        for other in range(2):
            chip = core * 8 + t
            target = (at["x"] * 2 + other, chip)
            me = jnp.logical_and(chip == zy, core == other)
            src = p_ref.at[16 * t : 16 * t + 16]
            dst = pas_rx.at[zy]
            k = t * 2 + other

            @pl.when(me)
            def _():
                pltpu.make_async_copy(src, dst, pas_recv.at[zy]).start()

            @pl.when(jnp.logical_not(me))
            def _():
                send(src, dst, pas_send.at[k], pas_recv.at[zy], target)

    for part in range(3):
        c, b, a = slot(part)
        buf = ags[part]
        axis = ORDERS[part][2]
        before, after = lax.rem(c + 3, 4), lax.rem(c + 1, 4)
        for j in range(4):
            bb = lax.rem(b + j, 4)
            k = part * 25 + 9 + 2 * j
            kf = part * 25 + 17 + j
            arrived(buf.at[0, before, bb], ag_recv.at[k])
            arrived(buf.at[0, after, bb], ag_recv.at[k + 1])
            view = buf.at[0, before if j < 2 else after, bb]
            pending.append(send(view, view, ag_send.at[kf], ag_recv.at[kf], peer(axis, 1 if j < 2 else 3)))
    for part in range(3):
        c, b, a = slot(part)
        second_arrived(part, 1)
        third(part, ags[part].at[1, c], part * 25 + 21)

    def forward_last():
        for part in range(3):
            c, b, a = slot(part)
            buf = ags[part]
            axis = ORDERS[part][2]
            before, after = lax.rem(c + 3, 4), lax.rem(c + 1, 4)
            k = part * 25 + 21
            arrived(buf.at[1, before], ag_recv.at[k])
            view = buf.at[1, before, 0:2]
            pending.append(send(view, view, ag_send.at[k + 2], ag_recv.at[k + 2], peer(axis, 1)))
            arrived(buf.at[1, after], ag_recv.at[k + 1])
            view = buf.at[1, after, 2:4]
            pending.append(send(view, view, ag_send.at[k + 3], ag_recv.at[k + 3], peer(axis, 3)))

    contract = (((1,), (1,)), ((), ()))

    def assemble(s):
        def one(i, _):
            z, y = i // 4, lax.rem(i, 4)
            for x in range(4):
                where = {"x": x, "y": y, "z": z}
                for part in range(3):
                    aa, bb, cc = ORDERS[part]
                    for row, rows, h, o in UNITS[part]:
                        start = s * HALF + x * 64 + row
                        cols = pl.ds(pl.multiple_of(i * 256 + 128 * h, 128), 128)
                        piece = ags[part][s, where[cc], where[bb], where[aa], o : o + rows]
                        queries[start : start + rows, cols] = piece
            return 0

        lax.fori_loop(0, 16, one, 0)

    mine = dp * 16 + mp
    theirs = (at["x"] * 2 + 1 - core) * 16 + mp
    sub = lax.broadcasted_iota(jnp.int32, (128, 128), 0)

    def find_names(s):
        for pair in range(2):
            pieces = []
            for x in (2 * pair, 2 * pair + 1):
                for i in range(8 * s, 8 * s + 8):
                    where = {"x": x, "y": i % 4, "z": i // 4}
                    aa, bb, cc = ORDERS[2]
                    tile = ag2[0, where[cc], where[bb], where[aa], 32:48].astype(F32)
                    pieces.append(tile[0:8] * 256.0 + tile[8:16])
            named = jnp.concatenate(pieces, axis=0).T[0:32].astype(jnp.int32)
            owner = named >> 9
            field = ((named >> 7) & 3) * 4
            bit = jnp.where(
                owner == mine, jnp.left_shift(1, field),
                jnp.where(owner == theirs, jnp.left_shift(1, field + 16), 0),
            )
            hi = named & 127
            packed = jnp.zeros((128, 128), jnp.int32)
            for k in range(NEGS):
                packed = packed + jnp.where(sub == hi[k : k + 1], bit[k : k + 1], 0)
            names[s, :, 128 * pair : 128 * pair + 128] = packed

    def score(s):
        rows = slice(s * HALF, s * HALF + HALF)

        def one(i, _):
            cols = pl.ds(pl.multiple_of(i * 2048, 2048), 2048)
            scores[s] += lax.dot_general(pool[:, cols], queries[rows, cols], contract, preferred_element_type=F32)
            return 0

        scores[s] = jnp.zeros((2 * ROWS + 16, HALF), F32)
        lax.fori_loop(0, 2, one, 0)

    lane = lax.broadcasted_iota(jnp.int32, (16, HALF), 1)
    psub = lax.broadcasted_iota(jnp.int32, (16, HALF), 0)
    in_plane = core == zy // 8
    row128 = lax.rem(zy, 8) * 16

    def same_of(s):
        held = jnp.logical_and(in_plane, row128 // 64 == s)
        first = jnp.where(held, at["x"] * 64 + lax.rem(row128, 64), -1024)
        return lane == first + psub

    def soften(s):
        def count_of(f):
            return (names[s] >> (4 * f)) & 15

        ps = scores[s, 2 * ROWS : 2 * ROWS + 16] * SCALE
        pos = jnp.sum(jnp.where(same_of(s), ps, 0.0), axis=0, keepdims=True)
        top = jnp.max(ps, axis=0, keepdims=True)
        for f in range(8):
            v = jnp.where(count_of(f) > 0, scores[s, 128 * f : 128 * f + 128] * SCALE, LOW)
            scores[s, 128 * f : 128 * f + 128] = v
            top = jnp.maximum(top, jnp.max(v, axis=0, keepdims=True))
        pe = jnp.exp(ps - top)
        scores[s, 2 * ROWS : 2 * ROWS + 16] = pe
        total = jnp.sum(pe, axis=0, keepdims=True)
        for f in range(8):
            e = jnp.exp(scores[s, 128 * f : 128 * f + 128] - top) * count_of(f).astype(F32)
            scores[s, 128 * f : 128 * f + 128] = e
            total = total + jnp.sum(e, axis=0, keepdims=True)
            et[s, :, 128 * f : 128 * f + 128] = e.T.astype(BF16)
        pet[s] = pe.T.astype(BF16)
        return top, total, pos

    filler = jnp.zeros((5, HALF), F32)

    def stats_send(s, n, tiles):
        for part in range(3):
            axis = ORDERS[part][2 - n]
            g = at[axis]
            stats[s, n, part, g] = jnp.concatenate(list(tiles[part]) + [filler], axis=0)
            ref = stats.at[s, n, part, g]
            for delta in (1, 2, 3):
                k = ((s * 3 + n) * 3 + part) * 3 + delta - 1
                pending.append(send(ref, ref, st_send.at[k], st_recv.at[k], peer(axis, delta)))

    def stats_meet(s, n):
        met = []
        for part in range(3):
            g = at[ORDERS[part][2 - n]]
            for delta in (1, 2, 3):
                k = ((s * 3 + n) * 3 + part) * 3 + delta - 1
                arrived(stats.at[s, n, part, lax.rem(g + 4 - delta, 4)], st_recv.at[k])
            tiles = [stats[s, n, part, j] for j in range(4)]
            best = tiles[0][0:1]
            for j in range(1, 4):
                best = jnp.maximum(best, tiles[j][0:1])
            summed = jnp.zeros_like(best)
            positive = jnp.zeros_like(best)
            for j in range(4):
                summed = summed + tiles[j][1:2] * jnp.exp(tiles[j][0:1] - best)
                positive = positive + tiles[j][2:3]
            met.append((best, summed, positive))
        return met

    third_part = lax.rem(lax.broadcasted_iota(jnp.int32, (1, HALF), 1), 64) >= 48

    def place_column(s, index, rows):
        for table, row in enumerate((jnp.where(third_part, rows[2], rows[0]), rows[1])):
            wide = jnp.broadcast_to(row, (128, HALF))
            for x in range(2):
                cols_of[s, index, table, 128 * x : 128 * x + 128] = wide[:, 128 * x : 128 * x + 128].T

    ds = (d0, d1, d2)

    def back(s):
        wide = 8

        def one(i, _):
            cols = pl.ds(pl.multiple_of(i * (256 * wide), 256 * wide), 256 * wide)
            acc = jnp.dot(et[s], pool[0 : 2 * ROWS, cols], preferred_element_type=F32)
            acc = (acc + jnp.dot(pet[s], pool[2 * ROWS : 2 * ROWS + 16, cols], preferred_element_type=F32)).astype(BF16)
            for j in range(wide):
                z, y = (i * wide + j) // 4, lax.rem(i * wide + j, 4)
                for x in range(4):
                    where = {"x": x, "y": y, "z": z}
                    for part in range(3):
                        aa, bb, cc = ORDERS[part]
                        for row, rows, h, o in UNITS[part]:
                            left = 256 * j + 128 * h
                            piece = acc[x * 64 + row : x * 64 + row + rows, left : left + 128]
                            ds[part][s, where[cc], where[bb], where[aa], o : o + rows] = piece
            return 0

        lax.fori_loop(0, 16 // wide, one, 0)

    hls, hrs, fls, frs = (hl0, hl1, hl2), (hr0, hr1, hr2), (fl0, fl1, fl2), (fr0, fr1, fr2)
    r1s, r2s = (r10, r11, r12), (r20, r21, r22)

    def scatter_key(part, s):
        return (part * 2 + s) * 12

    def scatter_start(s):
        for part in range(3):
            c, b, a = slot(part)
            axis = ORDERS[part][2]
            k = scatter_key(part, s)
            d = ds[part]
            far, before, after = lax.rem(c + 2, 4), lax.rem(c + 3, 4), lax.rem(c + 1, 4)
            right, left = peer(axis, 1), peer(axis, 3)
            pending.append(send(d.at[s, far, 0:2], hls[part].at[s], rs_send.at[k], rs_recv.at[k], right))
            pending.append(send(d.at[s, far, 2:4], hrs[part].at[s], rs_send.at[k + 1], rs_recv.at[k + 1], left))
            pending.append(send(d.at[s, after, 2:4], fls[part].at[s, 2:4], rs_send.at[k + 2], rs_recv.at[k + 2], right))
            pending.append(send(d.at[s, before, 0:2], frs[part].at[s, 0:2], rs_send.at[k + 3], rs_recv.at[k + 3], left))

    def factor_rows(part, s, index, c, b, a):
        x = dict(zip(ORDERS[part], (a, b, c)))["x"]
        if part < 2:
            return cols_of[s, index, part, pl.ds(pl.multiple_of(x * 64, 16), 48)]
        v = cols_of[s, index, 0, pl.ds(pl.multiple_of(x * 64 + 48, 16), 16)]
        return jnp.concatenate([v, v], axis=0)

    def scatter_forward(s):
        for part in range(3):
            c, b, a = slot(part)
            axis = ORDERS[part][2]
            k = scatter_key(part, s)
            d, hl, hr = ds[part], hls[part], hrs[part]
            before, after = lax.rem(c + 3, 4), lax.rem(c + 1, 4)

            def add(i, _, block, base, rx, column):
                bb, aa = i // 4, lax.rem(i, 4)
                own = d[s, block, base + bb, aa].astype(F32) * factor_rows(part, s, 0, block, base + bb, aa)
                other = rx[s, bb, aa].astype(F32) * factor_rows(part, s, column, block, base + bb, aa)
                d[s, block, base + bb, aa] = (own + other).astype(BF16)
                return 0

            arrived(hl.at[s], rs_recv.at[k])
            lax.fori_loop(0, 8, lambda i, t: add(i, t, after, 0, hl, 1), 0)
            pending.append(send(
                d.at[s, after, 0:2], fls[part].at[s, 0:2], rs_send.at[k + 4], rs_recv.at[k + 4], peer(axis, 1)
            ))
            arrived(hr.at[s], rs_recv.at[k + 1])
            lax.fori_loop(0, 8, lambda i, t: add(i, t, before, 2, hr, 2), 0)
            pending.append(send(
                d.at[s, before, 2:4], frs[part].at[s, 2:4], rs_send.at[k + 5], rs_recv.at[k + 5], peer(axis, 3)
            ))

    def scatter_second(s):
        for part in range(3):
            c, b, a = slot(part)
            k = scatter_key(part, s)
            d, fl, fr = ds[part], fls[part], frs[part]
            arrived(fl.at[s, 2:4], rs_recv.at[k + 2])
            arrived(fr.at[s, 0:2], rs_recv.at[k + 3])
            arrived(fl.at[s, 0:2], rs_recv.at[k + 4])
            arrived(fr.at[s, 2:4], rs_recv.at[k + 5])

            def low_half(i, _):
                bb, aa = i // 4, lax.rem(i, 4)
                total = d[s, c, bb, aa].astype(F32) * factor_rows(part, s, 0, c, bb, aa)
                total = total + fr[s, bb, aa].astype(F32) * factor_rows(part, s, 2, c, bb, aa) + fl[s, bb, aa].astype(F32)
                d[s, c, bb, aa] = (total * factor_rows(part, s, 3, c, bb, aa)).astype(BF16)
                return 0

            def high_half(i, _):
                bb, aa = i // 4 + 2, lax.rem(i, 4)
                total = d[s, c, bb, aa].astype(F32) * factor_rows(part, s, 0, c, bb, aa)
                total = total + fl[s, bb, aa].astype(F32) * factor_rows(part, s, 1, c, bb, aa) + fr[s, bb, aa].astype(F32)
                d[s, c, bb, aa] = (total * factor_rows(part, s, 3, c, bb, aa)).astype(BF16)
                return 0

            lax.fori_loop(0, 8, low_half, 0)
            lax.fori_loop(0, 8, high_half, 0)
            for delta in (1, 2, 3):
                pending.append(send(
                    d.at[s, c, lax.rem(b + delta, 4)], r1s[part].at[s, delta - 1],
                    rs_send.at[k + 5 + delta], rs_recv.at[k + 5 + delta], peer(ORDERS[part][1], delta),
                ))

    def scatter_third(s):
        for part in range(3):
            c, b, a = slot(part)
            k = scatter_key(part, s)
            d, r1 = ds[part], r1s[part]
            for delta in (1, 2, 3):
                arrived(r1.at[s, delta - 1], rs_recv.at[k + 5 + delta])
            for aa in range(4):
                total = d[s, c, b, aa].astype(F32)
                for j in range(3):
                    total = total + r1[s, j, aa].astype(F32)
                d[s, c, b, aa] = (total * factor_rows(part, s, 4, c, b, aa)).astype(BF16)
            for delta in (1, 2, 3):
                pending.append(send(
                    d.at[s, c, b, lax.rem(a + delta, 4)], r2s[part].at[s, delta - 1],
                    rs_send.at[k + 8 + delta], rs_recv.at[k + 8 + delta], peer(ORDERS[part][0], delta),
                ))

    def scatter_end(s):
        for part in range(3):
            c, b, a = slot(part)
            k = scatter_key(part, s)
            d, r2 = ds[part], r2s[part]
            total = d[s, c, b, a].astype(F32)
            for delta in (1, 2, 3):
                arrived(r2.at[s, delta - 1], rs_recv.at[k + 8 + delta])
                total = total + r2[s, delta - 1].astype(F32)
            total = total * factor_rows(part, s, 5, c, b, a)
            for row, rows, h, o in UNITS[part]:
                there = (slice(64 * s + row, 64 * s + row + rows), slice(128 * h, 128 * h + 128))
                gq_ref[there] = (total[o : o + rows] - p_ref[there].astype(F32) * (SCALE / BATCH)).astype(BF16)

    def first_factors(s, top, met):
        best = [met[part][0] for part in range(3)]
        place_column(s, 0, [jnp.exp(top - best[part]) for part in range(3)])
        for index, delta in ((1, 3), (2, 1)):
            rows = []
            for part in range(3):
                there = lax.rem(at[ORDERS[part][2]] + delta, 4)
                rows.append(jnp.exp(stats[s, 0, part, there][0:1] - best[part]))
            place_column(s, index, rows)

    def next_factors(s, index, met, wider):
        place_column(s, index, [jnp.exp(met[part][0] - wider[part][0]) for part in range(3)])

    def finish_stats(s, met, top):
        best, summed, positive = met[0]
        log_total = best + jnp.log(summed)
        place_column(s, 5, [jnp.exp(best - log_total) * (SCALE / BATCH)] * 3)
        return jnp.exp(top - log_total) / BATCH, jnp.sum(log_total - positive, axis=1, keepdims=True)

    def weigh(s, factor):
        own = slice(s * HALF, s * HALF + HALF)
        wp = scores[s, 2 * ROWS : 2 * ROWS + 16] * factor - jnp.where(same_of(s), 1.0 / BATCH, 0.0)
        wp = wp.astype(BF16)
        wx[0:ROWS, own] = (scores[s, ROWS : 2 * ROWS] * factor).astype(BF16)
        wx[ROWS : ROWS + 16, own] = wp
        wd[0:ROWS, own] = (scores[s, 0:ROWS] * factor).astype(BF16)
        wd[ROWS : ROWS + 16, own] = wp

    for part in range(3):
        c, b, a = slot(part)
        far = lax.rem(c + 2, 4)
        for j in range(4):
            arrived(ags[part].at[0, far, lax.rem(b + j, 4)], ag_recv.at[part * 25 + 17 + j])
    assemble(0)
    find_names(0)
    own_pool.wait()
    arrived(pool.at[ROWS : 2 * ROWS], pool_recv)
    for i in range(16):
        arrived(pas_rx.at[i], pas_recv.at[i])
        pool[2 * ROWS : 2 * ROWS + 16, 256 * i : 256 * i + 256] = pas_rx[i]
    score(0)
    forward_last()
    top_a, total_a, pos_a = soften(0)
    stats_send(0, 0, [(top_a, total_a, pos_a)] * 3)
    back(0)
    scatter_start(0)

    find_names(1)
    for part in range(3):
        c, b, a = slot(part)
        far = lax.rem(c + 2, 4)
        arrived(ags[part].at[1, far, 0:2], ag_recv.at[part * 25 + 23])
        arrived(ags[part].at[1, far, 2:4], ag_recv.at[part * 25 + 24])
    assemble(1)
    q_copy = send(queries.at[0:PLANE], queries.at[PLANE : 2 * PLANE], q_send, q_recv, sib)
    score(1)
    met_a1 = stats_meet(0, 0)
    stats_send(0, 1, met_a1)
    first_factors(0, top_a, met_a1)
    scatter_forward(0)
    top_b, total_b, pos_b = soften(1)
    stats_send(1, 0, [(top_b, total_b, pos_b)] * 3)
    back(1)
    scatter_start(1)

    met_a2 = stats_meet(0, 1)
    stats_send(0, 2, met_a2)
    next_factors(0, 3, met_a1, met_a2)
    scatter_second(0)
    met_b1 = stats_meet(1, 0)
    stats_send(1, 1, met_b1)
    first_factors(1, top_b, met_b1)
    scatter_forward(1)
    met_a3 = stats_meet(0, 2)
    next_factors(0, 4, met_a2, met_a3)
    factor_a, loss_a = finish_stats(0, met_a3, top_a)
    scatter_third(0)
    met_b2 = stats_meet(1, 1)
    stats_send(1, 2, met_b2)
    next_factors(1, 3, met_b1, met_b2)
    weigh(0, factor_a)
    scatter_second(1)
    met_b3 = stats_meet(1, 2)
    next_factors(1, 4, met_b2, met_b3)
    factor_b, loss_b = finish_stats(1, met_b3, top_b)
    weigh(1, factor_b)
    w_copy = send(wx, wd.at[:, PLANE : 2 * PLANE], w_send, w_recv, sib)
    loss_own[...] = jnp.broadcast_to(loss_a + loss_b, (8, 128))
    loss_copy = send(loss_own, loss_sib, loss_send, loss_recv, sib)

    arrived(queries.at[PLANE : 2 * PLANE], q_recv)
    arrived(wx, w_recv)

    def pool_grad(i, _):
        cols = pl.ds(pl.multiple_of(i * 512, 512), 512)
        acc = jnp.dot(wd[...], queries[:, cols], preferred_element_type=F32) * SCALE
        gpool_ref[:, cols] = acc[0:ROWS].astype(BF16)
        gp_tx[:, cols] = acc[ROWS : ROWS + 16].astype(BF16)
        return 0

    lax.fori_loop(0, 4, pool_grad, 0)
    scatter_third(1)
    lax.fori_loop(4, 8, pool_grad, 0)

    plane_of = zy // 8
    for t in range(8):
        there = core * 8 + t
        target = (at["x"] * 2 + plane_of, there)
        me = jnp.logical_and(there == zy, plane_of == core)
        src = gp_tx.at[:, pl.ds(pl.multiple_of(there * 256, 256), 256)]
        place = lax.rem(zy, 8)

        @pl.when(me)
        def _():
            pltpu.make_async_copy(src, gp_rx.at[place], gp_recv.at[place]).start()

        @pl.when(jnp.logical_not(me))
        def _():
            send(src, gp_rx.at[place], gp_send.at[t], gp_recv.at[place], target)

    scatter_end(0)
    scatter_end(1)

    for i in range(8):
        arrived(gp_rx.at[i], gp_recv.at[i])
        gp_ref[16 * i : 16 * i + 16] = gp_rx[i]
    arrived(loss_sib, loss_recv)
    loss_ref[...] = (loss_own[...] + loss_sib[...]) / BATCH

    for copy in pending:
        copy.wait_send()
    for copy in (pool_copy, q_copy, w_copy, loss_copy):
        copy.wait_send()
    for t in range(8):
        for other in range(2):
            chip = core * 8 + t
            me = jnp.logical_and(chip == zy, core == other)

            @pl.when(jnp.logical_not(me))
            def _():
                arrived(p_ref.at[16 * t : 16 * t + 16], pas_send.at[t * 2 + other])

        me = jnp.logical_and(core * 8 + t == zy, plane_of == core)

        @pl.when(jnp.logical_not(me))
        def _():
            arrived(gp_rx.at[0], gp_send.at[t])


def hand_on(loss_in, gq_in, gp_in, gpool_in, loss_out, gq_out, gp_out, gpool_out, sem):
    copies = [
        pltpu.make_async_copy(src, dst, sem.at[i])
        for i, (src, dst) in enumerate(((gpool_in, gpool_out), (gq_in, gq_out), (gp_in, gp_out)))
    ]
    for copy in copies:
        copy.start()
    loss_out[0, 0] = loss_in[0, 0]
    for copy in copies:
        copy.wait()


def body(queries, passages, pool_rows, negatives):
    vmem = pl.BlockSpec(memory_space=pltpu.VMEM)
    smem = pl.BlockSpec(memory_space=pltpu.SMEM)
    hbm = pl.BlockSpec(memory_space=pltpu.HBM)
    dma = pltpu.SemaphoreType.DMA
    pieces = jax.ShapeDtypeStruct((128, 256), BF16)
    rows_out = jax.ShapeDtypeStruct((ROWS, D), BF16)
    loss, gq, gp, gpool = pl.pallas_call(
        kernel,
        out_shape=(jax.ShapeDtypeStruct((8, 128), F32), pieces, pieces, rows_out),
        in_specs=[hbm, hbm, hbm, hbm],
        out_specs=(vmem, vmem, vmem, vmem),
        scratch_shapes=[
            pltpu.VMEM((128, 256), BF16),
            pltpu.VMEM((128, 256), BF16),
            pltpu.VMEM((8, NEGS), jnp.int32),
            dma((3,)),
            *[pltpu.VMEM((2, 4, 4, 4, AG_ROWS, 128), BF16)] * 3,
            pltpu.VMEM((2 * ROWS + 16, D), BF16),
            pltpu.VMEM((2 * PLANE, D), BF16),
            pltpu.VMEM((16, 16, 256), BF16),
            pltpu.VMEM((2, 2 * ROWS + 16, HALF), F32),
            pltpu.VMEM((2, 128, HALF), jnp.int32),
            pltpu.VMEM((2, HALF, 2 * ROWS), BF16),
            pltpu.VMEM((2, HALF, 16), BF16),
            pltpu.VMEM((ROWS + 16, 2 * PLANE), BF16),
            pltpu.VMEM((ROWS + 16, PLANE), BF16),
            pltpu.VMEM((2, 6, 2, HALF, 128), F32),
            pltpu.VMEM((2, 3, 3, 4, 8, HALF), F32),
            pltpu.VMEM((8, 128), F32),
            pltpu.VMEM((8, 128), F32),
            pltpu.VMEM((16, D), BF16),
            pltpu.VMEM((8, 16, 256), BF16),
            *[pltpu.VMEM((2, 4, 4, 4, rows, 128), BF16) for rows in RS_ROWS],
            *[pltpu.VMEM((2, 2, 4, rows, 128), BF16) for rows in RS_ROWS],
            *[pltpu.VMEM((2, 2, 4, rows, 128), BF16) for rows in RS_ROWS],
            *[pltpu.VMEM((2, 4, 4, rows, 128), BF16) for rows in RS_ROWS],
            *[pltpu.VMEM((2, 4, 4, rows, 128), BF16) for rows in RS_ROWS],
            *[pltpu.VMEM((2, 3, 4, rows, 128), BF16) for rows in RS_ROWS],
            *[pltpu.VMEM((2, 3, rows, 128), BF16) for rows in RS_ROWS],
            dma, dma, dma, dma((75,)), dma((75,)), dma((16,)), dma((16,)), dma, dma,
            dma((54,)), dma((54,)), dma, dma, dma((72,)), dma((72,)), dma((8,)), dma((8,)), dma, dma,
        ],
        compiler_params=pltpu.CompilerParams(
            collective_id=0, has_side_effects=True, vmem_limit_bytes=48 * 1024 * 1024
        ),
    )(queries, passages, pool_rows, negatives)
    loss, gq, gp, gpool = pl.pallas_call(
        hand_on,
        out_shape=(jax.ShapeDtypeStruct((1, 1), F32), pieces, pieces, rows_out),
        in_specs=[vmem, vmem, vmem, vmem],
        out_specs=(smem, hbm, hbm, hbm),
        scratch_shapes=[dma((3,))],
        compiler_params=pltpu.CompilerParams(vmem_limit_bytes=8 * 1024 * 1024),
    )(loss, gq, gp, gpool)
    return loss[0, 0], gq, gp, gpool


def solution(mesh):
    placed = (P("dp", "mp"), P("dp", "mp"), P(("dp", "mp"), None), P(("dp", "mp"), None))
    return jax.shard_map(
        body,
        mesh=mesh,
        in_specs=placed,
        out_specs=(P(), P("dp", "mp"), P("dp", "mp"), P(("dp", "mp"), None)),
        check_vma=False,
    )
```

time: 88.6 us -> 78.4 us (0.88)
  Pallas kernels: 87.7 us -> 75.2 us
  local copies, waits for them, and re-layouts: 0 us -> 2.36 us
    pallas_call x1, Pallas kernels: 81 us -> 72.6 us  [body(): pl.pallas_call(kernel, out_shape=(jax.ShapeDtypeStruct((8, 128), F32), pi...]
    pallas_call x1, Pallas kernels: 6.73 us -> 2.57 us  [body(): pl.pallas_call(hand_on, out_shape=(jax.ShapeDtypeStruct((1, 1), F32), pie...]
    unnamed x0 -> x6, local copies, waits for them, and re-layouts: none -> 2.36 us
where the time goes in v3:
time: 78.4 us; the launch traced here: 78.2 us
  Pallas kernels  75.2 us (96%)
  local copies, waits for them, and re-layouts  2.36 us (3%)
    pallas_call x1, Pallas kernels, body(): pl.pallas_call(kernel, out_shape=(jax.ShapeDtypeStruct((8, 128), F32), pi...  72.6 us
    pallas_call x1, Pallas kernels, body(): pl.pallas_call(hand_on, out_shape=(jax.ShapeDtypeStruct((1, 1), F32), pie...  2.57 us
    unnamed x6, local copies, waits for them, and re-layouts  2.36 us

profile of v3, /device:TPU:1, one launch (start us, length us, event | category | flops | bytes accessed | tf_op | source)
XLA Modules:
  0.0 78.2 jit_solution(6936162194858311070)
XLA Ops:
  0.6 0.0 copy-start
  0.6 0.8 %copy-done = bf16[128,256]{1,0:T(8,128)(2,1)S(1)} copy-done((bf16[128,256]{1,0:T(8,128)(2,1)S(1)}, bf16[128,256]{1,0:T(8,128)(2,1)}, u32[]{:S(2)}) %copy-start) | copy-done | bytes 65560
  1.5 0.0 copy-start.1
  1.5 0.8 %copy-done.1 = bf16[128,256]{1,0:T(8,128)(2,1)S(1)} copy-done((bf16[128,256]{1,0:T(8,128)(2,1)S(1)}, bf16[128,256]{1,0:T(8,128)(2,1)}, u32[]{:S(2)}) %copy-start.1) | copy-done | bytes 65560
  2.3 0.0 copy-start.2
  2.3 0.7 copy-done.2
  3.0 72.6 %shard_map.75 = (f32[8,128]{1,0:T(8,128)S(1)}, bf16[128,256]{1,0:T(8,128)(2,1)S(1)}, bf16[128,256]{1,0:T(8,128)(2,1)S(1)}, bf16[512,4096]{1,0:T(8,128)(2,1)S(1)}) custom-call(bf16[128,256]{1,0:T(8,128)(2,1)S(1)} %copy-done, bf16[128,256]{1,0:T(8,128)(2,1)S(1)} %copy-done.1, bf16[512,4096]{1,0:T(8,128)(2,1)} %pool_ref.1, s32[8,31]{1,0:T(8,128)S(1)} %copy-done.2), custom_call_target="tpu_custom_call" | custom-call | tf_op jit(solution)/shard_map/pallas_call | solution.py:620
  75.6 2.6 %shard_map.76 = (f32[1,1]{1,0:T(1,128)}, bf16[128,256]{1,0:T(8,128)(2,1)}, bf16[128,256]{1,0:T(8,128)(2,1)}, bf16[512,4096]{1,0:T(8,128)(2,1)}) custom-call(f32[8,128]{1,0:T(8,128)S(1)} %get-tuple-element.12.loss_in, bf16[128,256]{1,0:T(8,128)(2,1)S(1)} %get-tuple-element.13.gq_in, bf16[128,256]{1,0:T(8,128)(2,1)S(1)} %get-tuple-element.14.gp_in, ...), custom_call_target="tpu_custom_call" | custom-call | tf_op jit(solution)/shard_map/pallas_call | solution.py:660
Async XLA Ops:
  0.6 0.8 %copy-start = (bf16[128,256]{1,0:T(8,128)(2,1)S(1)}, bf16[128,256]{1,0:T(8,128)(2,1)}, u32[]{:S(2)}) copy-start(bf16[128,256]{1,0:T(8,128)(2,1)} %q_hbm.1) | copy-start | bytes 196612
  1.5 0.8 %copy-start.1 = (bf16[128,256]{1,0:T(8,128)(2,1)S(1)}, bf16[128,256]{1,0:T(8,128)(2,1)}, u32[]{:S(2)}) copy-start(bf16[128,256]{1,0:T(8,128)(2,1)} %p_hbm.1) | copy-start | bytes 196612
  2.3 0.7 copy-start.2

commit v4 on v3

--- a/solution.py
+++ b/solution.py
@@ -27,7 +27,7 @@
     q_hbm, p_hbm, pool_ref, neg_hbm,
     loss_ref, gq_ref, gp_ref, gpool_ref,
     q_ref, p_ref, neg_ref, in_sem, ag0, ag1, ag2, pool, queries, pas_rx, scores, names, et, pet, wd, wx, cols_of,
-    stats, loss_own, loss_sib, gp_tx, gp_rx,
+    stats, loss_own, loss_sib, gp_sum, gp_tx, gp_rx,
     d0, d1, d2, hl0, hl1, hl2, hr0, hr1, hr2, fl0, fl1, fl2, fr0, fr1, fr2, r10, r11, r12, r20, r21, r22,
     local_sem, pool_send, pool_recv, ag_send, ag_recv, pas_send, pas_recv, q_send, q_recv,
     st_send, st_recv, w_send, w_recv, rs_send, rs_recv, gp_send, gp_recv, loss_send, loss_recv,
@@ -194,7 +194,7 @@
                 for part in range(3):
                     aa, bb, cc = ORDERS[part]
                     for row, rows, h, o in UNITS[part]:
-                        start = s * HALF + x * 64 + row
+                        start = s * PLANE + x * 64 + row
                         cols = pl.ds(pl.multiple_of(i * 256 + 128 * h, 128), 128)
                         piece = ags[part][s, where[cc], where[bb], where[aa], o : o + rows]
                         queries[start : start + rows, cols] = piece
@@ -229,7 +229,7 @@
             names[s, :, 128 * pair : 128 * pair + 128] = packed
 
     def score(s):
-        rows = slice(s * HALF, s * HALF + HALF)
+        rows = slice(s * PLANE, s * PLANE + HALF)
 
         def one(i, _):
             cols = pl.ds(pl.multiple_of(i * 2048, 2048), 2048)
@@ -469,13 +469,37 @@
         return jnp.exp(top - log_total) / BATCH, jnp.sum(log_total - positive, axis=1, keepdims=True)
 
     def weigh(s, factor):
-        own = slice(s * HALF, s * HALF + HALF)
+        own = slice(s * PLANE, s * PLANE + HALF)
         wp = scores[s, 2 * ROWS : 2 * ROWS + 16] * factor - jnp.where(same_of(s), 1.0 / BATCH, 0.0)
         wp = wp.astype(BF16)
-        wx[0:ROWS, own] = (scores[s, ROWS : 2 * ROWS] * factor).astype(BF16)
-        wx[ROWS : ROWS + 16, own] = wp
+        wx[s, 0:ROWS] = (scores[s, ROWS : 2 * ROWS] * factor).astype(BF16)
+        wx[s, ROWS : ROWS + 16] = wp
         wd[0:ROWS, own] = (scores[s, 0:ROWS] * factor).astype(BF16)
         wd[ROWS : ROWS + 16, own] = wp
+
+    def there(s, plane):
+        return slice(s * PLANE + plane * HALF, s * PLANE + plane * HALF + HALF)
+
+    def weights_send(s):
+        return send(wx.at[s], wd.at[:, there(s, 1)], w_send.at[s], w_recv.at[s], sib)
+
+    def pool_grad(s):
+        arrived(queries.at[there(s, 1)], q_recv.at[s])
+        arrived(wx.at[s], w_recv.at[s])
+        both = slice(s * PLANE, s * PLANE + PLANE)
+
+        def one(i, _):
+            cols = pl.ds(pl.multiple_of(i * 1024, 1024), 1024)
+            acc = jnp.dot(wd[:, both], queries[both, cols], preferred_element_type=F32) * SCALE
+            if s == 0:
+                gpool_ref[:, cols] = acc[0:ROWS].astype(BF16)
+                gp_sum[:, cols] = acc[ROWS : ROWS + 16]
+            else:
+                gpool_ref[:, cols] = (gpool_ref[:, cols].astype(F32) + acc[0:ROWS]).astype(BF16)
+                gp_tx[:, cols] = (gp_sum[:, cols] + acc[ROWS : ROWS + 16]).astype(BF16)
+            return 0
+
+        lax.fori_loop(0, 4, one, 0)
 
     for part in range(3):
         c, b, a = slot(part)
@@ -503,7 +527,9 @@
         arrived(ags[part].at[1, far, 0:2], ag_recv.at[part * 25 + 23])
         arrived(ags[part].at[1, far, 2:4], ag_recv.at[part * 25 + 24])
     assemble(1)
-    q_copy = send(queries.at[0:PLANE], queries.at[PLANE : 2 * PLANE], q_send, q_recv, sib)
+    q_copies = [
+        send(queries.at[there(s, 0)], queries.at[there(s, 1)], q_send.at[s], q_recv.at[s], sib) for s in range(2)
+    ]
     score(1)
     met_a1 = stats_meet(0, 0)
     stats_send(0, 1, met_a1)
@@ -525,33 +551,23 @@
     met_a3 = stats_meet(0, 2)
     next_factors(0, 4, met_a2, met_a3)
     factor_a, loss_a = finish_stats(0, met_a3, top_a)
+    weigh(0, factor_a)
+    w_copies = [weights_send(0)]
     scatter_third(0)
     met_b2 = stats_meet(1, 1)
     stats_send(1, 2, met_b2)
     next_factors(1, 3, met_b1, met_b2)
-    weigh(0, factor_a)
+    pool_grad(0)
     scatter_second(1)
     met_b3 = stats_meet(1, 2)
     next_factors(1, 4, met_b2, met_b3)
     factor_b, loss_b = finish_stats(1, met_b3, top_b)
     weigh(1, factor_b)
-    w_copy = send(wx, wd.at[:, PLANE : 2 * PLANE], w_send, w_recv, sib)
+    w_copies.append(weights_send(1))
     loss_own[...] = jnp.broadcast_to(loss_a + loss_b, (8, 128))
     loss_copy = send(loss_own, loss_sib, loss_send, loss_recv, sib)
 
-    arrived(queries.at[PLANE : 2 * PLANE], q_recv)
-    arrived(wx, w_recv)
-
-    def pool_grad(i, _):
-        cols = pl.ds(pl.multiple_of(i * 512, 512), 512)
-        acc = jnp.dot(wd[...], queries[:, cols], preferred_element_type=F32) * SCALE
-        gpool_ref[:, cols] = acc[0:ROWS].astype(BF16)
-        gp_tx[:, cols] = acc[ROWS : ROWS + 16].astype(BF16)
-        return 0
-
-    lax.fori_loop(0, 4, pool_grad, 0)
-    scatter_third(1)
-    lax.fori_loop(4, 8, pool_grad, 0)
+    pool_grad(1)
 
     plane_of = zy // 8
     for t in range(8):
@@ -569,6 +585,7 @@
         def _():
             send(src, gp_rx.at[place], gp_send.at[t], gp_recv.at[place], target)
 
+    scatter_third(1)
     scatter_end(0)
     scatter_end(1)
 
@@ -580,7 +597,7 @@
 
     for copy in pending:
         copy.wait_send()
-    for copy in (pool_copy, q_copy, w_copy, loss_copy):
+    for copy in (pool_copy, loss_copy, *q_copies, *w_copies):
         copy.wait_send()
     for t in range(8):
         for other in range(2):
@@ -636,11 +653,12 @@
             pltpu.VMEM((2, HALF, 2 * ROWS), BF16),
             pltpu.VMEM((2, HALF, 16), BF16),
             pltpu.VMEM((ROWS + 16, 2 * PLANE), BF16),
-            pltpu.VMEM((ROWS + 16, PLANE), BF16),
+            pltpu.VMEM((2, ROWS + 16, HALF), BF16),
             pltpu.VMEM((2, 6, 2, HALF, 128), F32),
             pltpu.VMEM((2, 3, 3, 4, 8, HALF), F32),
             pltpu.VMEM((8, 128), F32),
             pltpu.VMEM((8, 128), F32),
+            pltpu.VMEM((16, D), F32),
             pltpu.VMEM((16, D), BF16),
             pltpu.VMEM((8, 16, 256), BF16),
             *[pltpu.VMEM((2, 4, 4, 4, rows, 128), BF16) for rows in RS_ROWS],
@@ -650,8 +668,8 @@
             *[pltpu.VMEM((2, 4, 4, rows, 128), BF16) for rows in RS_ROWS],
             *[pltpu.VMEM((2, 3, 4, rows, 128), BF16) for rows in RS_ROWS],
             *[pltpu.VMEM((2, 3, rows, 128), BF16) for rows in RS_ROWS],
-            dma, dma, dma, dma((75,)), dma((75,)), dma((16,)), dma((16,)), dma, dma,
-            dma((54,)), dma((54,)), dma, dma, dma((72,)), dma((72,)), dma((8,)), dma((8,)), dma, dma,
+            dma, dma, dma, dma((75,)), dma((75,)), dma((16,)), dma((16,)), dma((2,)), dma((2,)),
+            dma((54,)), dma((54,)), dma((2,)), dma((2,)), dma((72,)), dma((72,)), dma((8,)), dma((8,)), dma, dma,
         ],
         compiler_params=pltpu.CompilerParams(
             collective_id=0, has_side_effects=True, vmem_limit_bytes=48 * 1024 * 1024

time: 78.4 us -> 77.2 us (0.985)
  Pallas kernels: 75.2 us -> 74 us
    pallas_call x1, Pallas kernels: 72.6 us -> 71.4 us  [body(): pl.pallas_call(kernel, out_shape=(jax.ShapeDtypeStruct((8, 128), F32), pi...]
where the time goes in v4:
time: 77.2 us; the launch traced here: 77 us
  Pallas kernels  74 us (96%)
  local copies, waits for them, and re-layouts  2.36 us (3%)
    pallas_call x1, Pallas kernels, body(): pl.pallas_call(kernel, out_shape=(jax.ShapeDtypeStruct((8, 128), F32), pi...  71.4 us
    pallas_call x1, Pallas kernels, body(): pl.pallas_call(hand_on, out_shape=(jax.ShapeDtypeStruct((1, 1), F32), pie...  2.57 us
    unnamed x6, local copies, waits for them, and re-layouts  2.36 us

profile of v4, /device:TPU:1, one launch (start us, length us, event | category | flops | bytes accessed | tf_op | source)
XLA Modules:
  0.0 77.0 jit_solution(1294421331705658430)
XLA Ops:
  0.6 0.0 copy-start
  0.6 0.8 %copy-done = bf16[128,256]{1,0:T(8,128)(2,1)S(1)} copy-done((bf16[128,256]{1,0:T(8,128)(2,1)S(1)}, bf16[128,256]{1,0:T(8,128)(2,1)}, u32[]{:S(2)}) %copy-start) | copy-done | bytes 65560
  1.5 0.0 copy-start.1
  1.5 0.8 %copy-done.1 = bf16[128,256]{1,0:T(8,128)(2,1)S(1)} copy-done((bf16[128,256]{1,0:T(8,128)(2,1)S(1)}, bf16[128,256]{1,0:T(8,128)(2,1)}, u32[]{:S(2)}) %copy-start.1) | copy-done | bytes 65560
  2.3 0.0 copy-start.2
  2.3 0.7 copy-done.2
  3.0 71.4 %shard_map.75 = (f32[8,128]{1,0:T(8,128)S(1)}, bf16[128,256]{1,0:T(8,128)(2,1)S(1)}, bf16[128,256]{1,0:T(8,128)(2,1)S(1)}, bf16[512,4096]{1,0:T(8,128)(2,1)S(1)}) custom-call(bf16[128,256]{1,0:T(8,128)(2,1)S(1)} %copy-done, bf16[128,256]{1,0:T(8,128)(2,1)S(1)} %copy-done.1, bf16[512,4096]{1,0:T(8,128)(2,1)} %pool_ref.1, s32[8,31]{1,0:T(8,128)S(1)} %copy-done.2), custom_call_target="tpu_custom_call" | custom-call | tf_op jit(solution)/shard_map/pallas_call | solution.py:637
  74.4 2.6 %shard_map.76 = (f32[1,1]{1,0:T(1,128)}, bf16[128,256]{1,0:T(8,128)(2,1)}, bf16[128,256]{1,0:T(8,128)(2,1)}, bf16[512,4096]{1,0:T(8,128)(2,1)}) custom-call(f32[8,128]{1,0:T(8,128)S(1)} %get-tuple-element.12.loss_in, bf16[128,256]{1,0:T(8,128)(2,1)S(1)} %get-tuple-element.13.gq_in, bf16[128,256]{1,0:T(8,128)(2,1)S(1)} %get-tuple-element.14.gp_in, ...), custom_call_target="tpu_custom_call" | custom-call | tf_op jit(solution)/shard_map/pallas_call | solution.py:678
Async XLA Ops:
  0.6 0.8 %copy-start = (bf16[128,256]{1,0:T(8,128)(2,1)S(1)}, bf16[128,256]{1,0:T(8,128)(2,1)}, u32[]{:S(2)}) copy-start(bf16[128,256]{1,0:T(8,128)(2,1)} %q_hbm.1) | copy-start | bytes 196612
  1.5 0.8 %copy-start.1 = (bf16[128,256]{1,0:T(8,128)(2,1)S(1)}, bf16[128,256]{1,0:T(8,128)(2,1)}, u32[]{:S(2)}) copy-start(bf16[128,256]{1,0:T(8,128)(2,1)} %p_hbm.1) | copy-start | bytes 196612
  2.3 0.7 copy-start.2

commit v5 on v4

--- a/solution.py
+++ b/solution.py
@@ -232,12 +232,12 @@
         rows = slice(s * PLANE, s * PLANE + HALF)
 
         def one(i, _):
-            cols = pl.ds(pl.multiple_of(i * 2048, 2048), 2048)
+            cols = pl.ds(pl.multiple_of(i * 4096, 4096), 4096)
             scores[s] += lax.dot_general(pool[:, cols], queries[rows, cols], contract, preferred_element_type=F32)
             return 0
 
         scores[s] = jnp.zeros((2 * ROWS + 16, HALF), F32)
-        lax.fori_loop(0, 2, one, 0)
+        lax.fori_loop(0, 1, one, 0)
 
     lane = lax.broadcasted_iota(jnp.int32, (16, HALF), 1)
     psub = lax.broadcasted_iota(jnp.int32, (16, HALF), 0)
@@ -349,6 +349,13 @@
             right, left = peer(axis, 1), peer(axis, 3)
             pending.append(send(d.at[s, far, 0:2], hls[part].at[s], rs_send.at[k], rs_recv.at[k], right))
             pending.append(send(d.at[s, far, 2:4], hrs[part].at[s], rs_send.at[k + 1], rs_recv.at[k + 1], left))
+        for part in range(3):
+            c, b, a = slot(part)
+            axis = ORDERS[part][2]
+            k = scatter_key(part, s)
+            d = ds[part]
+            before, after = lax.rem(c + 3, 4), lax.rem(c + 1, 4)
+            right, left = peer(axis, 1), peer(axis, 3)
             pending.append(send(d.at[s, after, 2:4], fls[part].at[s, 2:4], rs_send.at[k + 2], rs_recv.at[k + 2], right))
             pending.append(send(d.at[s, before, 0:2], frs[part].at[s, 0:2], rs_send.at[k + 3], rs_recv.at[k + 3], left))
 
@@ -674,7 +681,7 @@
         compiler_params=pltpu.CompilerParams(
             collective_id=0, has_side_effects=True, vmem_limit_bytes=48 * 1024 * 1024
         ),
-    )(queries, passages, pool_rows, negatives)
+    )(*[pltpu.with_memory_space_constraint(v, pltpu.HBM) for v in (queries, passages, pool_rows, negatives)])
     loss, gq, gp, gpool = pl.pallas_call(
         hand_on,
         out_shape=(jax.ShapeDtypeStruct((1, 1), F32), pieces, pieces, rows_out),

time: 77.2 us -> 74.4 us (0.964)
  local copies, waits for them, and re-layouts: 2.36 us -> 0 us
    unnamed x6 -> x0, local copies, waits for them, and re-layouts: 2.36 us -> none
where the time goes in v5:
time: 74.4 us; the launch traced here: 74.3 us
  Pallas kernels  73.6 us (99%)
    pallas_call x1, Pallas kernels, body(): pl.pallas_call(kernel, out_shape=(jax.ShapeDtypeStruct((8, 128), F32), pi...  71 us
    pallas_call x1, Pallas kernels, body(): pl.pallas_call(hand_on, out_shape=(jax.ShapeDtypeStruct((1, 1), F32), pie...  2.57 us

profile of v5, /device:TPU:1, one launch (start us, length us, event | category | flops | bytes accessed | tf_op | source)
XLA Modules:
  0.0 74.3 jit_solution(12248498673402147449)
XLA Ops:
  0.6 71.0 %shard_map.75 = (f32[8,128]{1,0:T(8,128)S(1)}, bf16[128,256]{1,0:T(8,128)(2,1)S(1)}, bf16[128,256]{1,0:T(8,128)(2,1)S(1)}, bf16[512,4096]{1,0:T(8,128)(2,1)S(1)}) custom-call(bf16[128,256]{1,0:T(8,128)(2,1)} %q_hbm.1, bf16[128,256]{1,0:T(8,128)(2,1)} %p_hbm.1, bf16[512,4096]{1,0:T(8,128)(2,1)} %pool_ref.1, s32[8,31]{1,0:T(8,128)} %neg_hbm.1), custom_call_target="tpu_custom_call" | custom-call | tf_op jit(solution)/shard_map/pallas_call | solution.py:644
  71.7 2.6 %shard_map.76 = (f32[1,1]{1,0:T(1,128)}, bf16[128,256]{1,0:T(8,128)(2,1)}, bf16[128,256]{1,0:T(8,128)(2,1)}, bf16[512,4096]{1,0:T(8,128)(2,1)}) custom-call(f32[8,128]{1,0:T(8,128)S(1)} %get-tuple-element.12.loss_in, bf16[128,256]{1,0:T(8,128)(2,1)S(1)} %get-tuple-element.13.gq_in, bf16[128,256]{1,0:T(8,128)(2,1)S(1)} %get-tuple-element.14.gp_in, ...), custom_call_target="tpu_custom_call" | custom-call | tf_op jit(solution)/shard_map/pallas_call | solution.py:685
